TPU v7x, 32 devices: a whole 2x2x4 slice. The times are simulated.
32 devices in a mesh: seq: 8 (over y, x, core), fsdp: 4 (over z).
Axes of the slice: x: 2, y: 2, z: 4, core: 2. Of those that a mesh axis runs over, the one named last changes fastest.
Arguments:
- tokens: bfloat16 [8, 4096, 640], P('fsdp', 'seq'), may hold values from -6 to 6
- doc_starts: int32 [8, 4096], P('fsdp', 'seq'), may hold values from 0 to 1, as said below
- w_query: bfloat16 [640, 1024], P('fsdp'), may hold values from -0.25 to 0.25
- w_key: bfloat16 [640, 256], P('fsdp'), may hold values from -0.25 to 0.25
- w_value: bfloat16 [640, 256], P('fsdp'), may hold values from -0.25 to 0.25
- w_out: bfloat16 [1024, 640], P('fsdp'), may hold values from -1.5 to 1.5
- w_gate: bfloat16 [640, 2048], P('fsdp'), may hold values from -0.25 to 0.25
- w_up: bfloat16 [640, 2048], P('fsdp'), may hold values from -0.25 to 0.25
- w_down: bfloat16 [2048, 640], P('fsdp'), may hold values from -0.125 to 0.125
- pre_attn: float32 [640], replicated, may hold values from 0.25 to 1.75
- post_attn: float32 [640], replicated, may hold values from 0.25 to 1.75
- pre_ffn: float32 [640], replicated, may hold values from 0.25 to 1.75
- post_ffn: float32 [640], replicated, may hold values from 0.25 to 1.75
- query_norm: float32 [256], replicated, may hold values from 0.25 to 1.75
- key_norm: float32 [256], replicated, may hold values from 0.25 to 1.75
- cotangent: bfloat16 [8, 4096, 640], P('fsdp', 'seq'), may hold values from -6 to 6
Outputs:
- layer_out: bfloat16 [8, 4096, 640], P('fsdp', 'seq')
- dtokens: bfloat16 [8, 4096, 640], P('fsdp', 'seq')
- dw_query: float32 [640, 1024], P('fsdp', 'seq')
- dw_key: float32 [640, 256], P('fsdp', 'seq')
- dw_value: float32 [640, 256], P('fsdp', 'seq')
- dw_out: float32 [1024, 640], P('fsdp', 'seq')
- dw_gate: float32 [640, 2048], P('fsdp', 'seq')
- dw_up: float32 [640, 2048], P('fsdp', 'seq')
- dw_down: float32 [2048, 640], P('fsdp', 'seq')
- dpre_attn: float32 [640], replicated
- dpost_attn: float32 [640], replicated
- dpre_ffn: float32 [640], replicated
- dpost_ffn: float32 [640], replicated
- dquery_norm: float32 [256], replicated
- dkey_norm: float32 [256], replicated
Inputs may be any that keep to these rules, and one draw needn't show every extreme that they name: `doc_starts`: 1 marks the first token of a document, 0 any other token; the first token of every sequence is 1.
All inputs are finite; a program needn't handle non-finite values.
Results may differ from a plain program's by a relative error of at most 0.022.
Values may be sent and summed in bfloat16 or wider, within the bound.
No kernel may reach another device: no remote copies, remote signals or barrier semaphores. Data moves between devices by JAX's collectives and lax.ppermute only.
A program may use at most 192 MiB of HBM per device.

v0:
```python
import jax
import jax.numpy as jnp
import numpy as np
from jax import lax
from jax.experimental import pallas as pl
from jax.experimental.pallas import tpu as pltpu
from jax.sharding import PartitionSpec as P

WINDOW = 512
TILE = 128
FF_TILE = 256
FFN_ROWS = 256

epsilon = 1e-06
NEG_FILL = -1e30
ROPE_BASE = 10000.0
GELU_C = 0.7978845608028654
GELU_K = 0.044715

f32 = jnp.float32
bf16 = jnp.bfloat16

NN = (((1,), (0,)), ((), ()))
NT = (((1,), (1,)), ((), ()))
TN = (((0,), (0,)), ((), ()))


def mm(left, right, dims=NN):
    return lax.dot_general(left, right, dims, preferred_element_type=f32)


def inv_rms(vector):
    return lax.rsqrt(jnp.mean(vector * vector, axis=-1, keepdims=True) + epsilon)


def norm_back(vector, inv, gain, grad):
    unit = vector * inv
    scaled = gain * grad
    back = inv * (scaled - unit * jnp.mean(unit * scaled, axis=-1, keepdims=True))
    return back, grad * unit


def rope(vector, cosine, sine):
    half = vector.shape[-1] // 2
    one, two = vector[:, :half], vector[:, half:]
    return jnp.concatenate([one * cosine - two * sine, two * cosine + one * sine], axis=1)


def rope_back(vector, cosine, sine):
    half = vector.shape[-1] // 2
    one, two = vector[:, :half], vector[:, half:]
    return jnp.concatenate([one * cosine + two * sine, two * cosine - one * sine], axis=1)


def params(limit_mib=58):
    return pltpu.CompilerParams(vmem_limit_bytes=limit_mib * 1024 * 1024)


def cost(microseconds):
    return pl.CostEstimate(
        flops=int(microseconds * 1e9), bytes_accessed=int(microseconds * 3e6), transcendentals=0
    )


def whole(shape):
    return pl.BlockSpec(shape, lambda *_: (0,) * len(shape))


def rows(count, width):
    return pl.BlockSpec((count, width), lambda i: (i, 0))


def shaped(shape, dtype):
    return jax.ShapeDtypeStruct(shape, dtype)


def qkv_kernel(
    held_ref, tok_ref, far_ref, cos_ref, sin_ref, gains_ref, head_ref, *refs
):
    packs = refs[:-9]
    attn_ref, qraw_ref, qrot_ref, kraw_ref, key_ref, val_ref, wq_ref, wkv_ref, wot_ref = refs[-9:]
    head_dim = head_ref.shape[1]
    head_count = wq_ref.shape[1] // head_dim
    block, width = tok_ref.shape
    chunks, chunk_rows, _ = packs[0].shape
    pieces = len(packs)
    half = pieces // 2

    @pl.when(pl.program_id(0) == 0)
    def _():
        strip = chunk_rows // 2
        odd = held_ref[0] % 2 == 1

        def aligned(index, size):
            return pl.ds(pl.multiple_of(index * size, size), size)

        for c in range(chunks):
            z = held_ref[pieces + c]
            own = aligned(z, chunk_rows)
            for m in range(pieces):
                s = held_ref[m]
                wq_ref[own, aligned(s, 128)] = packs[m][c, :, :128]
                turned = packs[m][c, :, 128:256]
                for i in range(2):
                    wot_ref[aligned(s, strip), aligned(2 * z + i, 128)] = turned[
                        i * strip : (i + 1) * strip
                    ]
            for m, mate in zip(range(half), (0, 2, 1, 3)):
                one, two = packs[m][c, :, 256:320], packs[half + mate][c, :, 256:320]
                wkv_ref[own, aligned(held_ref[m] // 2, 128)] = jnp.concatenate(
                    [jnp.where(odd, two, one), jnp.where(odd, one, two)], axis=1
                )

    pre = gains_ref[0:1, :]
    qgain, kgain = head_ref[0:1, :], head_ref[1:2, :]
    token = tok_ref[...].astype(f32)
    low = (token * inv_rms(token) * pre).astype(bf16)
    attn_ref[...] = low
    query = mm(low, wq_ref[...])
    qraw_ref[...] = query
    cosine, sine = cos_ref[block:, :], sin_ref[block:, :]
    scaling = head_dim ** (-0.5)
    for h in range(head_count):
        part = query[:, h * head_dim : (h + 1) * head_dim]
        normed = part * inv_rms(part) * qgain
        qrot_ref[:, h * head_dim : (h + 1) * head_dim] = (
            rope(normed, cosine, sine).astype(bf16) * jnp.asarray(scaling, bf16)
        )
    both = mm(low, wkv_ref[...])
    key = both[:, :head_dim]
    kraw_ref[...] = key
    key_ref[0, block:, :] = rope(key * inv_rms(key) * kgain, cosine, sine).astype(bf16)
    val_ref[0, block:, :] = both[:, head_dim:].astype(bf16)
    token = far_ref[...].astype(f32)
    low = (token * inv_rms(token) * pre).astype(bf16)
    both = mm(low, wkv_ref[...])
    key = both[:, :head_dim]
    key_ref[0, :block, :] = rope(
        key * inv_rms(key) * kgain, cos_ref[:block, :], sin_ref[:block, :]
    ).astype(bf16)
    val_ref[0, :block, :] = both[:, head_dim:].astype(bf16)


def stacked(ref, tile, head_count, head_dim):
    return jnp.concatenate(
        [
            ref[tile * TILE : (tile + 1) * TILE, h * head_dim : (h + 1) * head_dim]
            for h in range(head_count)
        ],
        axis=0,
    )


def mask_of(pos_ref, tile, span):
    reach = pos_ref[tile * TILE : (tile + 1) * TILE, :]
    row = lax.broadcasted_iota(jnp.int32, (TILE, span), 0)
    col = lax.broadcasted_iota(jnp.int32, (TILE, span), 1)
    distance = WINDOW + row - col
    return jnp.where((distance >= 0) & (distance <= reach), 0.0, NEG_FILL)


def attn_kernel(
    q_ref, key_ref, val_ref, pos_ref, tok_ref, wot_ref, gains_ref,
    ctx_ref, lse_ref, branch_ref, res_ref, fin_ref,
):
    head_dim = key_ref.shape[2]
    head_count = q_ref.shape[1] // head_dim
    span = WINDOW + TILE
    lane = lax.broadcasted_iota(jnp.int32, (TILE, 128), 1)
    for tile in range(q_ref.shape[0] // TILE):
        query = stacked(q_ref, tile, head_count, head_dim)
        key = key_ref[0, tile * TILE : tile * TILE + span, :]
        value = val_ref[0, tile * TILE : tile * TILE + span, :]
        score = mm(query, key, NT).reshape(head_count, TILE, span) + mask_of(pos_ref, tile, span)
        largest = jnp.max(score, axis=-1, keepdims=True)
        expo = jnp.exp(score - largest)
        total = jnp.sum(expo, axis=-1, keepdims=True)
        low = expo.astype(bf16).reshape(head_count * TILE, span)
        context = mm(low, value).reshape(head_count, TILE, head_dim) / total
        log_total = largest + jnp.log(total)
        kept = jnp.zeros((TILE, 128), f32)
        for h in range(head_count):
            ctx_ref[tile * TILE : (tile + 1) * TILE, h * head_dim : (h + 1) * head_dim] = context[
                h
            ].astype(bf16)
            kept = jnp.where(lane == h, log_total[h], kept)
        lse_ref[tile * TILE : (tile + 1) * TILE, :] = kept
    branch = mm(ctx_ref[...], wot_ref[...], NT)
    branch_ref[...] = branch
    residual = tok_ref[...].astype(f32) + branch * inv_rms(branch) * gains_ref[1:2, :]
    res_ref[...] = residual
    fin_ref[...] = (residual * inv_rms(residual) * gains_ref[2:3, :]).astype(bf16)


def ffn_kernel(
    held_ref, order_ref, res_ref, fin_ref, cot_ref, branch_ref, ctx_ref, wot_ref, gains_ref, *refs
):
    pieces = order_ref.shape[0] - refs[0].shape[0]
    packs, refs = refs[:pieces], refs[pieces:]
    out_ref, gres_ref, gctx_ref, gain_ref = refs[:4]
    gate_sent, gate_kept, down_sent, down_kept = refs[4:8]
    slope_ref, act_ref, gate_ref, up_ref, down_ref, stage_ref, copied = refs[8:15]
    hid_ref, gg_ref, gu_ref, in_left, ffn_left, attn_left, turn_ref = refs[15:]
    chunks, _, tile = packs[0].shape
    width = res_ref.shape[1]
    count = hid_ref.shape[0]
    quarter, strip, half = width // chunks, width // pieces, pieces // 2
    step = pl.program_id(0)
    tiles = count // FFN_ROWS
    post_attn, pre_ffn, post_ffn = [gains_ref[i : i + 1, :] for i in (1, 2, 3)]

    def aligned(index, size):
        return pl.ds(pl.multiple_of(index * size, size), size)

    @pl.when(step == 0)
    def _():
        gain_ref[...] = jnp.zeros_like(gain_ref)

        def staged(m):
            return pltpu.make_async_copy(packs[m], stage_ref.at[m % 2], copied.at[m % 2])

        staged(0).start()
        for m in range(pieces):
            if m + 1 < pieces:
                staged(m + 1).start()
            staged(m).wait()
            s = held_ref[m]
            for c in range(chunks):
                z = held_ref[pieces + c]
                own, cols = aligned(z, quarter), aligned(s, tile)
                gate_ref[own, cols] = stage_ref[m % 2, c, :quarter, :]
                up_ref[own, cols] = stage_ref[m % 2, c, quarter : 2 * quarter, :]
                for i in range(2):
                    begin = 2 * quarter + i * strip
                    down_ref[aligned(s, strip), aligned(2 * z + i, tile)] = stage_ref[
                        m % 2, c, begin : begin + strip, :
                    ]

    @pl.when(step < tiles)
    def _():
        own = aligned(step, FFN_ROWS)

        def turn(left_ref, source, size, first, number):
            turn_ref[...] = source.T
            for m in range(number):
                left_ref[m * size : (m + 1) * size, own] = turn_ref[
                    aligned(order_ref[first + m], size), :
                ]

        ffn_in = fin_ref[...]
        turn(in_left, ffn_in, quarter, pieces, chunks)
        gate = mm(ffn_in, gate_ref[...])
        up = mm(ffn_in, up_ref[...])
        square = gate * gate
        bent = jnp.tanh(GELU_C * gate * (1.0 + GELU_K * square))
        half_bent = 0.5 * (1.0 + bent)
        act = gate * half_bent
        slope = half_bent + 0.5 * gate * (1.0 - bent * bent) * (
            GELU_C * (1.0 + 3.0 * GELU_K * square)
        )
        act_ref[...] = act
        slope_ref[...] = slope * up
        hidden = (act * up).astype(bf16)
        hid_ref[own, :] = hidden
        branch = mm(hidden, down_ref[...], NT)
        residual = res_ref[...]
        cot = cot_ref[...].astype(f32)
        inv = inv_rms(branch)
        out_ref[...] = (residual + branch * inv * post_ffn).astype(bf16)
        g_ffn, gain_post = norm_back(branch, inv, post_ffn, cot)
        g_low = g_ffn.astype(bf16)
        turn(ffn_left, g_low, strip, 0, pieces)
        g_hidden = mm(g_low, down_ref[...])
        g_gate = (g_hidden * slope_ref[...]).astype(bf16)
        g_up = (g_hidden * act_ref[...]).astype(bf16)
        gg_ref[own, :] = g_gate
        gu_ref[own, :] = g_up
        g_in = mm(g_gate, gate_ref[...], NT) + mm(g_up, up_ref[...], NT)
        back, gain_pre = norm_back(residual, inv_rms(residual), pre_ffn, g_in)
        g_res = cot + back
        gres_ref[...] = g_res
        attn_branch = branch_ref[...]
        g_attn, gain_attn = norm_back(attn_branch, inv_rms(attn_branch), post_attn, g_res)
        g_attn = g_attn.astype(bf16)
        turn(attn_left, g_attn, strip, 0, pieces)
        gctx_ref[...] = mm(g_attn, wot_ref[...]).astype(bf16)
        gain_ref[0:1, :] += jnp.sum(gain_post, axis=0, keepdims=True)
        gain_ref[1:2, :] += jnp.sum(gain_pre, axis=0, keepdims=True)
        gain_ref[2:3, :] += jnp.sum(gain_attn, axis=0, keepdims=True)

    @pl.when(step >= tiles)
    def _():
        k = step - tiles
        cols = aligned(order_ref[k], tile)
        z = order_ref[pieces + k // 2]
        both = mm(in_left[...], jnp.concatenate([gg_ref[:, cols], gu_ref[:, cols]], axis=1))
        both = both.astype(bf16)
        for i in range(2):
            part = both[:, i * tile : (i + 1) * tile].reshape(chunks, quarter, tile)
            for inside, out in ((k < half, gate_sent), (k >= half, gate_kept)):

                @pl.when(inside)
                def _(out=out, part=part, i=i):
                    out[0, :, i * quarter : (i + 1) * quarter, :] = part

        def put(begin, part):
            part = part.astype(bf16).reshape(pieces, strip, tile)
            down_sent[:, 0, pl.ds(begin, strip), :] = part[:half]
            down_kept[:, 0, pl.ds(begin, strip), :] = part[half:]

        put(
            pl.multiple_of(k % 2 * strip, strip),
            mm(ffn_left[...], hid_ref[:, aligned(2 * z + k % 2, tile)]),
        )

        @pl.when(k % 2 == 0)
        def _():
            put(2 * strip, mm(attn_left[...], ctx_ref[:, aligned(z, tile)]))


def turn_strips(left_ref, source, strip, where, count):
    left_ref[1] = source.T
    for m in range(count):
        begin = pl.multiple_of(where(m) * strip, 16)
        left_ref[0, m * strip : (m + 1) * strip, :] = left_ref[1, pl.ds(begin, strip), :]


def attn_grad_kernel(base, order_ref, _, attn_ref, gq_ref, gkv_ref, sort_ref, *refs):
    recv_ref = refs[0] if base else None
    outs = refs[1:3] if base else refs[:1]
    left = refs[-1]
    held, chunks, quarter, _ = outs[0].shape
    width = attn_ref.shape[1]
    pieces = order_ref.shape[0] - chunks
    half = pieces // 2
    turn_strips(left, attn_ref[...], quarter, lambda m: order_ref[pieces + m], chunks)
    sorted_kv = mm(gkv_ref[...], sort_ref[...]).astype(bf16)
    part_kv = mm(left[0], sorted_kv)
    wide = part_kv.shape[1] // half
    for pair in range(0, half, 2):
        both = jnp.concatenate(
            [
                gq_ref[:, pl.ds(pl.multiple_of(order_ref[base + pair + i] * 128, 128), 128)]
                for i in range(2)
            ],
            axis=1,
        )
        part = mm(left[0], both)
        for i in range(2):
            m = pair + i
            value = part[:, i * 128 : (i + 1) * 128].reshape(chunks, quarter, 128)
            value_kv = part_kv[:, m * wide : (m + 1) * wide].reshape(chunks, quarter, wide)
            if base:
                value = value + recv_ref[m, :, :, :128].astype(f32)
                value_kv = value_kv + recv_ref[m, :, :, 128:].astype(f32)
            out = outs[m // held]
            out[m % held, :, :, :128] = value.astype(bf16)
            out[m % held, :, :, 128:] = value_kv.astype(bf16)


def attn_back_kernel(
    q_ref, gctx_ref, key_ref, val_ref, pos_ref, lse_ref, qraw_ref, cos_ref, sin_ref, head_ref,
    gq_ref, far_ref, near_ref, gain_ref, gkey_ref, gval_ref,
):
    head_dim = key_ref.shape[2]
    head_count = q_ref.shape[1] // head_dim
    block = q_ref.shape[0]
    span = WINDOW + TILE
    scaling = head_dim ** (-0.5)

    @pl.when(pl.program_id(0) == 0)
    def _():
        gain_ref[...] = jnp.zeros_like(gain_ref)

    gkey_ref[...] = jnp.zeros_like(gkey_ref)
    gval_ref[...] = jnp.zeros_like(gval_ref)
    gain = jnp.zeros((1, head_dim), f32)
    for tile in range(block // TILE):
        own = slice(tile * TILE, (tile + 1) * TILE)
        reach = slice(tile * TILE, tile * TILE + span)
        query = stacked(q_ref, tile, head_count, head_dim)
        g_ctx = stacked(gctx_ref, tile, head_count, head_dim)
        key = key_ref[0, reach, :]
        value = val_ref[0, reach, :]
        log_total = jnp.stack([lse_ref[own, h : h + 1] for h in range(head_count)])
        score = mm(query, key, NT).reshape(head_count, TILE, span) + mask_of(pos_ref, tile, span)
        probs = jnp.exp(score - log_total)
        g_probs = mm(g_ctx, value, NT).reshape(head_count, TILE, span)
        spread = jnp.sum(g_probs * probs, axis=-1, keepdims=True)
        g_score = (probs * (g_probs - spread)).astype(bf16).reshape(head_count * TILE, span)
        low = probs.astype(bf16).reshape(head_count * TILE, span)
        gkey_ref[reach, :] += mm(g_score, query, TN)
        gval_ref[reach, :] += mm(low, g_ctx, TN)
        g_rot = mm(g_score, key) * scaling
        turned = slice(block + tile * TILE, block + (tile + 1) * TILE)
        cosine, sine = cos_ref[turned, :], sin_ref[turned, :]
        for h in range(head_count):
            cols = slice(h * head_dim, (h + 1) * head_dim)
            raw = qraw_ref[own, cols]
            back, share = norm_back(
                raw,
                inv_rms(raw),
                head_ref[0:1, :],
                rope_back(g_rot[h * TILE : (h + 1) * TILE], cosine, sine),
            )
            gq_ref[own, cols] = back.astype(bf16)
            gain += jnp.sum(share, axis=0, keepdims=True)
    gain_ref[0:1, :] += gain
    far_ref[0, :, :head_dim] = rope_back(
        gkey_ref[:block, :], cos_ref[:block, :], sin_ref[:block, :]
    ).astype(bf16)
    far_ref[0, :, head_dim:] = gval_ref[:block, :].astype(bf16)
    near_ref[0, :, :head_dim] = gkey_ref[block:, :]
    near_ref[0, :, head_dim:] = gval_ref[block:, :]


def kv_back_kernel(
    kraw_ref, cos_ref, sin_ref, head_ref, near_ref, recv_ref, _, gkv_ref, kgain_ref
):
    head_dim = head_ref.shape[1]

    @pl.when(pl.program_id(0) == 0)
    def _():
        kgain_ref[...] = jnp.zeros_like(kgain_ref)

    near, far = near_ref[0], recv_ref[0].astype(f32)
    raw = kraw_ref[...]
    g_normed = rope_back(near[:, :head_dim], cos_ref[...], sin_ref[...]) + far[:, :head_dim]
    g_key, share = norm_back(raw, inv_rms(raw), head_ref[1:2, :], g_normed)
    kgain_ref[0:1, :] += jnp.sum(share, axis=0, keepdims=True)
    gkv_ref[:, :head_dim] = g_key.astype(bf16)
    gkv_ref[:, head_dim:] = (near[:, head_dim:] + far[:, head_dim:]).astype(bf16)


def input_kernel(
    _, __, gq_ref, gkv_ref, wq_ref, wkv_ref, tok_ref, gres_ref, gains_ref, ffn_gain_ref, kgain_ref,
    qgain_ref, dtok_ref, gain_ref
):
    @pl.when(pl.program_id(0) == 0)
    def _():
        gain_ref[...] = jnp.zeros_like(gain_ref)
        head_dim = kgain_ref.shape[1]
        gain_ref[1:4, :] = ffn_gain_ref[0:3, :]
        gain_ref[4:5, :head_dim] = qgain_ref[0:1, :]
        gain_ref[4:5, head_dim : 2 * head_dim] = kgain_ref[0:1, :]

    g_in = mm(gq_ref[...], wq_ref[...], NT) + mm(gkv_ref[...], wkv_ref[...], NT)
    token = tok_ref[...].astype(f32)
    back, share = norm_back(token, inv_rms(token), gains_ref[0:1, :], g_in)
    dtok_ref[...] = (gres_ref[...] + back).astype(bf16)
    gain_ref[0:1, :] += jnp.sum(share, axis=0, keepdims=True)


def passed_along(shard, axis, by):
    length = lax.axis_size(axis)
    pairs = [(i, i + by) for i in range(length) if 0 <= i + by < length]
    return lax.ppermute(shard, axis, pairs)


def swapped(array, axis, even, odd):
    length = lax.axis_size(axis)
    return lax.ppermute(array, axis, [(i, i ^ (odd if i % 2 else even)) for i in range(length)])


def tables(block, head_dim):
    half_width = head_dim // 2
    frequency = ROPE_BASE ** (-(np.arange(half_width) * 2.0) / head_dim)
    angles = np.arange(-block, block)[:, None] * frequency
    return np.cos(angles).astype(np.float32), np.sin(angles).astype(np.float32)


def column_piece(array, axis_name, parts):
    wide = array.shape[1] // parts
    return lax.dynamic_slice_in_dim(array, lax.axis_index(axis_name) * wide, wide, 1)


def halves(array):
    if isinstance(array, tuple):
        return tuple(zip(*(halves(part) for part in array)))
    half = array.shape[0] // 2
    return (array[:half], array[half:]) if half > 1 else (array[0], array[1])


def total(terms):
    laid = [term for term in terms if isinstance(term, tuple)]
    terms = [term for term in terms if not isinstance(term, tuple)]
    if laid:
        terms.insert(0, jnp.concatenate([total(list(parts)) for parts in zip(*laid)], axis=-2))
    result = terms[0].astype(f32)
    for term in terms[1:]:
        result = result + term.astype(f32)
    return result


HELD = [0, 4, 2, 6, 1, 3, 5, 7]
HELD_Z = [0, 2, 1, 3]


def linked(*chains):
    arrays, steps = [], []
    for chain in chains:
        send, keep = chain if isinstance(chain, tuple) else (chain, [])
        arrays.append([send] + [array for array, _ in keep])
        steps.append([begin for _, begin in keep])
    arrays = lax.optimization_barrier(arrays)
    result = []
    for chain, (send, *keep), begins in zip(chains, arrays, steps):
        result.append((send, list(zip(keep, begins))) if isinstance(chain, tuple) else send)
    return result


class Exchange:
    def __init__(self, seqs, chunks):
        self.direct = seqs == 8 and chunks == 4
        if not self.direct:
            self.order = jnp.arange(12, dtype=jnp.int32) % 8
            self.held = jnp.array(HELD + HELD_Z, jnp.int32)
            return
        s, z = lax.axis_index("seq"), lax.axis_index("fsdp")
        odd = s % 2 == 1
        one, two = jnp.where(odd, 4, 2), jnp.where(odd, 2, 4)
        zero = jnp.zeros_like(s)
        sent = [one | two | 1, two | 1, one | 1, zero | 1]
        kept = [one | two, one, two, zero]
        order = [s ^ k for k in sent + kept] + [z ^ k for k in (3, 1, 2, 0)]
        self.order = jnp.stack(order).astype(jnp.int32)
        held = [zero, two, one, one | two, zero | 1, one | 1, two | 1, one | two | 1]
        held = [s ^ k for k in held] + [z ^ k for k in HELD_Z]
        self.held = jnp.stack(held).astype(jnp.int32)

    def along_step(self, held, bits):
        return jnp.concatenate([held, swapped(held, "fsdp", bits, bits)], axis=0)

    def second(self, piece):
        return swapped(piece, "seq", 4, 2)

    def first(self, piece):
        return swapped(piece, "seq", 2, 4)

    def swap_cores(self, parts):
        return swapped(parts, "seq", 1, 1)

    def fold(self, send, keep, step):
        if step < 3:
            got = swapped(send, "seq", *((1, 1), (2, 4), (4, 2))[step])
        else:
            got = swapped(send, "fsdp", step - 2, step - 2)
        return self.split(keep + [(got, step)], step)

    def split(self, terms, step):
        rest = []
        for array, begin in terms:
            for done in range(begin, step):
                array = halves(array)[1]
            rest.append(array)
        if step == 4:
            return total(rest)
        return total([halves(array)[0] for array in rest]).astype(bf16), terms

    def hop_terms(self, send, keep):
        keep = keep + [(swapped(send, "seq", 4, 2), 2)]
        rest = []
        for array, begin in keep:
            for done in range(begin, 2):
                array = halves(array)[1]
            rest.append(array)
        parts = [total([array[p] for array in rest]) for p in range(4)]
        return [part.astype(bf16) for part in parts[:3]] + [parts[3]]

    def last(self, *parts):
        got = [swapped(part, "fsdp", bits, bits) for part, bits in zip(parts, (3, 1, 2))]
        return total([parts[3]] + got)

    def hop(self, value, axis, bits):
        got = [swapped(value, axis, b, b) for b in bits]
        if len(bits) == 1:
            return value + got[0]
        both = bits[0] | bits[1]
        return (value + got[0]) + (got[1] + swapped(value, axis, both, both))


def scattered_plain(part):
    columns = lax.psum_scatter(part, "seq", scatter_dimension=1, tiled=True)
    return lax.psum_scatter(columns, "fsdp", scatter_dimension=0, tiled=True).astype(f32)


def gather_weights(w_query, w_key, w_value, w_out, w_gate, w_up, w_down, halo, exchange):
    pieces = w_gate.shape[1] // FF_TILE
    width = w_out.shape[1]
    if exchange.direct:
        down = column_piece(w_down, "seq", pieces).T
        ffn = jnp.concatenate(
            [
                column_piece(w_gate, "seq", pieces),
                column_piece(w_up, "seq", pieces),
                down[:, :FF_TILE],
                down[:, FF_TILE:],
            ],
            axis=0,
        )
        both = jnp.concatenate([w_key, w_value], axis=1)
        out = column_piece(w_out, "seq", pieces).T
        out = jnp.concatenate([out[:, :128], out[:, 128:]], axis=0)
        attn = jnp.concatenate(
            [column_piece(w_query, "seq", pieces), out, column_piece(both, "seq", pieces)], axis=1
        )
        attn = exchange.along_step(exchange.along_step(attn[None], 2), 1)
        ffn, attn = lax.optimization_barrier((ffn, attn))
        ffn = exchange.along_step(ffn[None], 2)
        attn, halo = lax.optimization_barrier((attn, halo))
        two, one = exchange.second(attn), exchange.first(attn)
        ffn, two = lax.optimization_barrier((ffn, two))
        ffn = exchange.along_step(ffn, 1)
        attn = [attn, two, one, exchange.first(two)]
        attn[3], ffn = lax.optimization_barrier((attn[3], ffn))
        return attn + [exchange.swap_cores(held) for held in attn], ffn, halo
    w_query, w_key, w_value, w_out, w_gate, w_up, w_down = [
        lax.all_gather(w, "fsdp", axis=0, tiled=True)
        for w in (w_query, w_key, w_value, w_out, w_gate, w_up, w_down)
    ]
    chunks = w_down.shape[0] // (2 * FF_TILE)
    quarter, strip = width // chunks, width // pieces

    def columns(weight):
        return weight.reshape(chunks, quarter, pieces, -1).transpose(2, 0, 1, 3)

    def turned(weight):
        shape = (pieces, strip, chunks, 2, weight.shape[0] // (2 * chunks))
        turned_part = weight.T.reshape(shape).transpose(0, 2, 3, 1, 4)
        return turned_part.reshape(pieces, chunks, 2 * strip, -1)

    both = jnp.concatenate([w_key, w_value], axis=1)
    attn = jnp.concatenate([columns(w_query), turned(w_out), columns(both)], axis=3)
    ffn = jnp.concatenate([columns(w_gate), columns(w_up), turned(w_down)], axis=2)
    def listed(pack):
        pack = jnp.take(jnp.take(pack, np.array(HELD), axis=0), np.array(HELD_Z), axis=1)
        return [pack[m] for m in range(pieces)]

    return listed(attn), listed(ffn), halo


def plain_gradients(part_gate, part_down, part_attn):
    pieces, quarters, double, _ = part_gate.shape
    width = quarters * double // 2
    strip = width // pieces

    def columns(parts):
        return parts.transpose(1, 2, 0, 3).reshape(width, -1)

    def turned(parts):
        parts = parts.reshape(pieces, quarters, -1, strip, FF_TILE).transpose(1, 2, 4, 0, 3)
        return parts.reshape(-1, width)

    each = part_attn.shape[3] - (part_attn.shape[3] - 128) // 2
    return tuple(
        scattered_plain(part)
        for part in (
            columns(part_attn[..., :128]),
            columns(part_attn[..., 128:each]),
            columns(part_attn[..., each:]),
            turned(part_down[:, :, 2 * strip :]),
            columns(part_gate[:, :, : double // 2]),
            columns(part_gate[:, :, double // 2 :]),
            turned(part_down[:, :, : 2 * strip]),
        )
    )


def split_gradients(ffn, attn):
    quarter = attn.shape[0]
    gate, down = ffn[: 2 * quarter], ffn[2 * quarter :]
    strip = down.shape[0] // 3
    each = attn.shape[1] - (attn.shape[1] - 128) // 2
    return (
        attn[:, :128],
        attn[:, 128:each],
        attn[:, each:],
        down[2 * strip :].T,
        gate[:quarter],
        gate[quarter:],
        jnp.concatenate([down[:strip].T, down[strip : 2 * strip].T], axis=0),
    )


def body(
    tokens, doc_starts, w_query, w_key, w_value, w_out, w_gate, w_up, w_down,
    pre_attn, post_attn, pre_ffn, post_ffn, query_norm, key_norm, cotangent,
):
    seq_dev, block, width = tokens.shape
    head_dim = w_key.shape[1]
    inner = w_query.shape[1]
    hidden_dim = w_gate.shape[1]
    count = seq_dev * block
    seqs, chunks = lax.axis_size("seq"), lax.axis_size("fsdp")
    exchange = Exchange(seqs, chunks)
    far_tokens = passed_along(tokens, "seq", 1).reshape(count, width)
    far_starts = passed_along(doc_starts, "seq", 1)
    pack, ffn_pack, (far_tokens, far_starts) = gather_weights(
        w_query, w_key, w_value, w_out, w_gate, w_up, w_down, (far_tokens, far_starts), exchange
    )
    starts = jnp.concatenate([far_starts, doc_starts], axis=1)
    indices = jnp.arange(2 * block, dtype=jnp.int32)
    latest = lax.cummax(jnp.where(starts == 1, indices[None, :], -WINDOW), axis=1)
    reach = jnp.minimum(indices[None, :] - latest, WINDOW - 1)[:, block:]
    pos_column = reach.reshape(count, 1)
    cosine, sine = tables(block, head_dim)
    own_cosine, own_sine = cosine[block:], sine[block:]

    pieces, quarters = len(pack), pack[0].shape[0]
    quarter, strip = width // quarters, width // pieces
    gains = jnp.stack([pre_attn, post_attn, pre_ffn, post_ffn])
    head_gains = jnp.stack([query_norm, key_norm])
    tokens_2d = tokens.reshape(count, width)
    cot_2d = cotangent.reshape(count, width)

    tok_spec = rows(block, width)
    table_spec = whole((2 * block, head_dim // 2))
    half_spec = whole((block, head_dim // 2))
    key_spec = pl.BlockSpec((1, 2 * block, head_dim), lambda i: (i, 0, 0))
    gains_spec, head_spec = whole((4, width)), whole((2, head_dim))
    wq_spec, wkv_spec, wot_spec = (
        whole((width, inner)),
        whole((width, 2 * head_dim)),
        whole((width, inner)),
    )
    smem = pl.BlockSpec(memory_space=pltpu.SMEM)
    remain = pl.BlockSpec(memory_space=pl.ANY)
    attn_low, query_raw, query_rot, key_raw, keys, values, full_q, full_kv, full_ot = (
        pl.pallas_call(
            qkv_kernel,
            grid=(seq_dev,),
            in_specs=[smem, tok_spec, tok_spec, table_spec, table_spec]
            + [gains_spec, head_spec]
            + [whole(pack[0].shape)] * pieces,
            out_specs=[
                tok_spec,
                rows(block, inner),
                rows(block, inner),
                rows(block, head_dim),
                key_spec,
                key_spec,
                wq_spec,
                wkv_spec,
                wot_spec,
            ],
            out_shape=[
                shaped((count, width), bf16),
                shaped((count, inner), f32),
                shaped((count, inner), bf16),
                shaped((count, head_dim), f32),
                shaped((seq_dev, 2 * block, head_dim), bf16),
                shaped((seq_dev, 2 * block, head_dim), bf16),
                shaped((width, inner), bf16),
                shaped((width, 2 * head_dim), bf16),
                shaped((width, inner), bf16),
            ],
            compiler_params=params(),
            name="project_rotate",
        cost_estimate=cost(11),
        )(
            exchange.held, tokens_2d, far_tokens, cosine, sine, gains, head_gains,
            *pack,
        )
    )
    if exchange.direct:
        own, two = ffn_pack, exchange.second(ffn_pack)
        own_swapped = exchange.swap_cores(own)
        again, two, keys = lax.optimization_barrier((own, two, keys))
        one, both, two_swapped = exchange.first(again), exchange.first(two), exchange.swap_cores(two)
    context, log_total, attn_branch, residual, ffn_in = pl.pallas_call(
        attn_kernel,
        grid=(seq_dev,),
        in_specs=[rows(block, inner), key_spec, key_spec, rows(block, 1), tok_spec]
        + [wot_spec, gains_spec],
        out_specs=[rows(block, inner), rows(block, 128), tok_spec, tok_spec, tok_spec],
        out_shape=[
            shaped((count, inner), bf16),
            shaped((count, 128), f32),
            shaped((count, width), f32),
            shaped((count, width), f32),
            shaped((count, width), bf16),
        ],
        compiler_params=params(),
        name="window_attention",
        cost_estimate=cost(12),
    )(query_rot, keys, values, pos_column, tokens_2d, full_ot, gains)

    if exchange.direct:
        one, both, ffn_in = lax.optimization_barrier((one, both, ffn_in))
        ffn_pack = [own, two, one, both, own_swapped, two_swapped]
        ffn_pack += [exchange.swap_cores(one), exchange.swap_cores(both)]

    half = pieces // 2
    tiles = count // FFN_ROWS

    def small(wide):
        return pl.BlockSpec((FFN_ROWS, wide), lambda i: (jnp.minimum(i, tiles - 1), 0))

    def once(shape):
        return pl.BlockSpec(
            shape, lambda *_: (0,) * len(shape), pipeline_mode=pl.Buffered(buffer_count=1)
        )

    gate_shape = (half, quarters, 2 * quarter, FF_TILE)
    down_shape = (half, quarters, 3 * strip, FF_TILE)

    def gate_spec(first):
        return pl.BlockSpec(
            (1,) + gate_shape[1:],
            lambda i: (jnp.clip(i - tiles - first, 0, half - 1), 0, 0, 0),
        )

    down_spec = pl.BlockSpec(
        (half, 1) + down_shape[2:], lambda i: (0, jnp.clip(i - tiles, 0, pieces - 1) // 2, 0, 0)
    )
    turned = pltpu.VMEM((width, count), bf16)
    weight = pltpu.VMEM((width, hidden_dim), bf16)
    middle = pltpu.VMEM((count, hidden_dim), bf16)
    gelu_parts = pltpu.VMEM((FFN_ROWS, hidden_dim), f32)
    layer_out, g_res, g_ctx, ffn_gains, *ffn_parts = pl.pallas_call(
        ffn_kernel,
        grid=(tiles + pieces,),
        in_specs=[smem, smem, small(width), small(width), small(width), small(width)]
        + [once((count, inner)), once((width, inner)), gains_spec]
        + [remain] * pieces,
        out_specs=[small(width), small(width), small(inner), whole((8, width))]
        + [gate_spec(0), gate_spec(half), down_spec, down_spec],
        out_shape=[
            shaped((count, width), bf16),
            shaped((count, width), f32),
            shaped((count, inner), bf16),
            shaped((8, width), f32),
            shaped(gate_shape, bf16),
            shaped(gate_shape, bf16),
            shaped(down_shape, bf16),
            shaped(down_shape, bf16),
        ],
        scratch_shapes=[gelu_parts, gelu_parts, weight, weight, weight]
        + [pltpu.VMEM((2,) + ffn_pack[0].shape, bf16), pltpu.SemaphoreType.DMA((2,))]
        + [middle, middle, middle, turned, turned, turned]
        + [pltpu.VMEM((width, FFN_ROWS), bf16)],
        compiler_params=params(62),
        name="feed_forward",
        cost_estimate=cost(60),
    )(
        exchange.held, exchange.order, residual, ffn_in, cot_2d, attn_branch, context, full_ot,
        gains, *ffn_pack,
    )
    gate_sent, gate_kept, down_sent, down_kept = ffn_parts
    gate, down = (gate_sent, gate_kept), (down_sent, down_kept)
    if exchange.direct:
        gate_got, down_got = swapped(gate_sent, "seq", 1, 1), swapped(down_sent, "seq", 1, 1)


    pair = pl.BlockSpec((1, block, 2 * head_dim), lambda i: (i, 0, 0))
    g_query, g_far, g_near, query_gain = pl.pallas_call(
        attn_back_kernel,
        grid=(seq_dev,),
        in_specs=[rows(block, inner), rows(block, inner), key_spec, key_spec]
        + [rows(block, 1), rows(block, 128), rows(block, inner), table_spec, table_spec]
        + [head_spec],
        out_specs=[rows(block, inner), pair, pair, whole((8, head_dim))],
        out_shape=[
            shaped((count, inner), bf16),
            shaped((seq_dev, block, 2 * head_dim), bf16),
            shaped((seq_dev, block, 2 * head_dim), f32),
            shaped((8, head_dim), f32),
        ],
        scratch_shapes=[
            pltpu.VMEM((2 * block, head_dim), f32),
            pltpu.VMEM((2 * block, head_dim), f32),
        ],
        compiler_params=params(),
        name="attention_gradient",
        cost_estimate=cost(16),
    )(
        query_rot, g_ctx, keys, values, pos_column, log_total, query_raw, cosine, sine,
        head_gains,
    )
    g_recv = passed_along(g_far, "seq", -1)
    ffn = ffn_parts
    if exchange.direct:
        gate_got, down_got, g_query = lax.optimization_barrier((gate_got, down_got, g_query))
        kept, got = (gate_kept, down_kept), (gate_got, down_got)
        ffn = exchange.split([(kept, 0), (got, 0)], 0)
    g_kv, key_gain = pl.pallas_call(
        kv_back_kernel,
        grid=(seq_dev,),
        in_specs=[rows(block, head_dim), half_spec, half_spec, head_spec]
        + [pair, pair, remain],
        out_specs=[rows(block, 2 * head_dim), whole((8, head_dim))],
        out_shape=[shaped((count, 2 * head_dim), bf16), shaped((8, head_dim), f32)],
        compiler_params=params(),
        name="key_value_back",
        cost_estimate=cost(4),
    )(key_raw, own_cosine, own_sine, head_gains, g_near, g_recv, ffn[0])

    each = head_dim // pieces
    column = jnp.arange(2 * head_dim, dtype=jnp.int32)
    inside = column % (2 * each)
    source = jnp.where(inside < each, inside, inside - each + head_dim)
    source = source + each * jnp.repeat(exchange.order[:pieces], 2 * each)
    sort = (column[:, None] == source[None, :]).astype(bf16)

    def attn_parts(base, before, extra):
        shape = (half, quarters, quarter, 128 + 2 * each)
        sent = (half // 2,) + shape[1:]
        outs = [shape] if base == 0 else [sent, sent]
        vmem = pl.BlockSpec(memory_space=pltpu.VMEM)
        chosen = sort[:, base * 2 * each : (base + half) * 2 * each]
        return pl.pallas_call(
            lambda *refs: attn_grad_kernel(base, *refs),
            in_specs=[smem, remain] + [vmem] * (4 + len(extra)),
            out_specs=[vmem] * len(outs),
            out_shape=[shaped(o, bf16) for o in outs],
            scratch_shapes=[pltpu.VMEM((2, width, count), bf16)],
            compiler_params=params(),
            cost_estimate=cost(6),
            name="attn_gradients_kept" if base else "attn_gradients_sent",
        )(exchange.order, before, attn_low, g_query, g_kv, chosen, *extra)

    early = ffn
    if exchange.direct:
        ffn = early = exchange.fold(*ffn, 1)
    (attn_sent,) = attn_parts(0, early[0], [])
    attn_got = exchange.swap_cores(attn_sent) if exchange.direct else jnp.zeros_like(attn_sent)
    if exchange.direct:
        ffn = exchange.fold(*ffn, 2)
    attn_parts_kept = attn_parts(half, ffn[0], [attn_got])
    attn = attn_parts_kept[0], [(attn_parts_kept[1], 1)]
    if exchange.direct:
        ffn, attn = linked(exchange.fold(*ffn, 3), exchange.fold(*attn, 1))
    dtokens, sums = pl.pallas_call(
        input_kernel,
        grid=(seq_dev,),
        in_specs=[remain, remain, rows(block, inner), rows(block, 2 * head_dim)]
        + [wq_spec, wkv_spec]
        + [tok_spec, tok_spec, gains_spec, whole((8, width))]
        + [whole((8, head_dim))] * 2,
        out_specs=[tok_spec, whole((8, width))],
        out_shape=[shaped((count, width), bf16), shaped((8, width), f32)],
        compiler_params=params(),
        name="input_gradient",
        cost_estimate=cost(7),
    )(ffn[0], attn[0], g_query, g_kv, full_q, full_kv, tokens_2d, g_res, gains, ffn_gains, key_gain, query_gain)

    if exchange.direct:
        attn = exchange.hop_terms(*attn)
        sums = exchange.hop(sums, "seq", (1,))
        *attn, sums = linked(*attn, sums)
        attn = exchange.last(*attn)
        sums = exchange.hop(sums, "seq", (2, 4))
        ffn = exchange.fold(*ffn, 4)
        ffn, attn, sums = linked(ffn, attn, sums)
        sums = exchange.hop(sums, "fsdp", (1, 2))
        weights = split_gradients(ffn, attn)
    else:
        weights = plain_gradients(
            jnp.concatenate(gate, axis=0),
            jnp.concatenate(down, axis=0),
            jnp.concatenate([attn_sent, *attn_parts_kept], axis=0),
        )
        sums = lax.psum(sums, ("seq", "fsdp"))
    gain_sums = (sums[0], sums[3], sums[2], sums[1])
    gain_sums += (sums[4, :head_dim], sums[4, head_dim : 2 * head_dim])
    shape = (seq_dev, block, width)
    return (layer_out.reshape(shape), dtokens.reshape(shape)) + weights + gain_sums


def solution(mesh):
    sharded = P("fsdp", "seq", None)
    weight = P("fsdp", None)
    in_specs = (sharded, P("fsdp", "seq")) + (weight,) * 7 + (P(),) * 6 + (sharded,)
    out_specs = (sharded, sharded) + (P("fsdp", "seq"),) * 7 + (P(),) * 6
    return jax.shard_map(body, mesh=mesh, in_specs=in_specs, out_specs=out_specs, check_vma=False)
```

profile of v0, /device:TPU:0, one launch (start us, length us, event | category | flops | bytes accessed | tf_op | source)
XLA Modules:
  0.0 312.7 jit_solution(12831797875658283353)
XLA Ops:
  0.7 2.6 collective-permute-start.2
  6.1 3.5 %collective-permute-start = (bf16[1,160,320]{2,1,0:T(8,128)(2,1)S(1)}, bf16[1,160,320]{2,1,0:T(8,128)(2,1)S(1)}, u32[]{:S(2)}, u32[]{:S(2)}) collective-permute-start(bf16[1,160,320]{2,1,0:T(8,128)(2,1)S(1)} %maximum_bitcast_fusion), channel_id=1, source_target_pairs={{0,2},{1,3},{2,0},{3,1},{4,6},{5,7},{6,4},{7,5},{8,10},{9,11},{10,... | collective-permute-start | bytes 307208 | tf_op jit(solution)/shard_map/ppermute | solution.py:462
  9.6 3.3 %collective-permute-start.3 = (s32[2,512]{1,0:T(2,128)}, s32[2,512]{1,0:T(2,128)S(1)}, u32[]{:S(2)}, u32[]{:S(2)}) collective-permute-start(s32[2,512]{1,0:T(2,128)} %param.21), channel_id=1, source_target_pairs={{0,4},{4,8},{8,12},{12,16},{16,20},{20,24},{24,28},{1,5},{5,9},{9,... | collective-permute-start | bytes 12296 | tf_op jit(solution)/shard_map/ppermute | solution.py:457
  13.2 2.2 collective-permute-done
  18.4 5.8 %collective-permute-done.1 = bf16[2,160,320]{2,1,0:T(8,128)(2,1)S(1)} collective-permute-done((bf16[2,160,320]{2,1,0:T(8,128)(2,1)S(1)}, bf16[2,160,320]{2,1,0:T(8,128)(2,1)S(1)}, u32[]{:S(2)}, u32[]{:S(2)}) %collective-permute-start.1) | collective-permute-done | bytes 204832 | tf_op jit(solution)/shard_map/ppermute | solution.py:462
  24.4 2.3 collective-permute-start.5
  26.7 2.3 collective-permute-start.4
  29.7 10.0 %collective-permute-done.4 = bf16[1,480,256]{2,1,0:T(8,128)(2,1)S(1)} collective-permute-done((bf16[1,480,256]{2,1,0:T(8,128)(2,1)S(1)}, bf16[1,480,256]{2,1,0:T(8,128)(2,1)S(1)}, u32[]{:S(2)}, u32[]{:S(2)}) %collective-permute-start.4) | collective-permute-done | bytes 245792 | tf_op jit(solution)/shard_map/ppermute | solution.py:462
  45.8 4.9 %collective-permute-done.6.refs_2_ = bf16[4,160,320]{2,1,0:T(8,128)(2,1)} collective-permute-done((bf16[4,160,320]{2,1,0:T(8,128)(2,1)S(1)}, bf16[4,160,320]{2,1,0:T(8,128)(2,1)}, u32[]{:S(2)}, u32[]{:S(2)}) %collective-permute-start.6) | collective-permute-done | bytes 409632 | tf_op jit(solution)/shard_map/ppermute | solution.py:462
  50.7 2.1 collective-permute-done.8
  52.9 3.1 collective-permute-done.7.refs_3_
  58.8 11.0 %project_rotate.1 = (bf16[1024,640]{1,0:T(8,128)(2,1)}, f32[1024,1024]{1,0:T(8,128)}, bf16[1024,1024]{1,0:T(8,128)(2,1)}, f32[1024,256]{1,0:T(8,128)}, bf16[2,10...) custom-call(s32[12]{0:T(128)} %stack.92.held_ref, ...), custom_call_target="tpu_custom_call" | custom-call | flops 11000000512 | bytes 33000000 | tf_op jit(solution)/shard_map/project_rotate/pallas_call | solution.py:729
  73.4 12.1 %window_attention.1 = (bf16[1024,1024]{1,0:T(8,128)(2,1)}, f32[1024,128]{1,0:T(8,128)}, f32[1024,640]{1,0:T(8,128)}, f32[1024,640]{1,0:T(8,128)}, bf16[1024,640]{1,0:T(8,128)(2,1)}) custom-call(bf16[1024,1024]{1,0:T(8,128)(2,1)} %get-tuple-element.91.q_ref, bf16[2,1024,256]{2,1,0:T(8,128)(2,1)} %get-tuple-element.94.key_ref, ...), custom_call_target="tpu_custom_call" | custom-call | flops 12000000000 | bytes 36000000 | tf_op jit(solution)/shard_map/window_attention/pallas_call | solution.py:770
  85.5 10.8 %collective-permute-done.14.refs_2_ = bf16[4,480,256]{2,1,0:T(8,128)(2,1)} collective-permute-done((bf16[4,480,256]{2,1,0:T(8,128)(2,1)S(1)}, bf16[4,480,256]{2,1,0:T(8,128)(2,1)}, u32[]{:S(2)}, u32[]{:S(2)}) %collective-permute-start.14) | collective-permute-done | bytes 983072 | tf_op jit(solution)/shard_map/ppermute | solution.py:462
  97.5 2.4 collective-permute-done.18.refs_6_
  100.4 64.1 %feed_forward.1 = (bf16[1024,640]{1,0:T(8,128)(2,1)}, f32[1024,640]{1,0:T(8,128)}, bf16[1024,1024]{1,0:T(8,128)(2,1)}, f32[8,640]{1,0:T(8,128)}, bf16[4,4,320,25...) custom-call(s32[12]{0:T(128)} %stack.92.held_ref, ...), custom_call_target="tpu_custom_call" | custom-call | flops 60000002048 | bytes 180000000 | tf_op jit(solution)/shard_map/feed_forward/pallas_call | solution.py:820
  165.1 16.4 %attention_gradient.1 = (bf16[1024,1024]{1,0:T(8,128)(2,1)}, bf16[2,512,512]{2,1,0:T(8,128)(2,1)}, f32[2,512,512]{2,1,0:T(8,128)}, f32[8,256]{1,0:T(8,128)}) custom-call(bf16[1024,1024]{1,0:T(8,128)(2,1)} %get-tuple-element.91.q_ref, bf16[1024,1024]{1,0:T(8,128)(2,1)} %get-tuple-element.111.gctx_ref, bf16[2,1024,256]{2,1,0:T(8,128)(2,1)} %get-tuple-element.94.key_ref, ...), custom_call_target="tpu_custom_call" | custom-call | flops 16000000000 | bytes 48000000 | tf_op jit(solution)/shard_map/attention_gradient/pallas_call | solution.py:856
  192.5 3.8 %key_value_back.1 = (bf16[1024,512]{1,0:T(8,128)(2,1)}, f32[8,256]{1,0:T(8,128)}) custom-call(f32[1024,256]{1,0:T(8,128)} %get-tuple-element.120.kraw_ref, f32[512,128]{1,0:T(8,128)} %constant.82.clone.cos_ref, f32[512,128]{1,0:T(8,128)} %constant.83.clone.sin_ref, f32[2,256]{1,0:T(2,128)} %pad_maximum_fusion.8.head_ref, ...), custom_call_target="tpu_custom_call" | custom-call | flops 4000000000 | bytes 12000000 | tf_op jit(solution)/shard_map/key_value_back/pallas_call | solution.py:886
  196.3 19.1 %collective-permute-done.22 = bf16[2,4,560,256]{3,2,1,0:T(8,128)(2,1)} collective-permute-done((bf16[2,4,560,256]{3,2,1,0:T(8,128)(2,1)}, bf16[2,4,560,256]{3,2,1,0:T(8,128)(2,1)}, u32[]{:S(2)}, u32[]{:S(2)}) %collective-permute-start.22) | collective-permute-done | bytes 2293792 | tf_op jit(solution)/shard_map/ppermute | solution.py:462
  215.4 2.5 fusion.refs_1_
  218.0 14.5 %collective-permute-start.23 = (bf16[4,560,256]{2,1,0:T(8,128)(2,1)}, bf16[4,560,256]{2,1,0:T(8,128)(2,1)S(1)}, u32[]{:S(2)}, u32[]{:S(2)}) collective-permute-start(bf16[4,560,256]{2,1,0:T(8,128)(2,1)} %fusion.refs_1_), channel_id=1, source_target_pairs={{0,16},{4,12},{8,24},{12,4},{16,0},{20,28},{24,8},{28,20},{1,17},{... | collective-permute-start | bytes 3440648 | tf_op jit(solution)/shard_map/ppermute | solution.py:462
  232.5 5.5 %attn_gradients_sent.1 = bf16[4,4,160,192]{3,2,1,0:T(8,128)(2,1)} custom-call(s32[12]{0:T(128)} %stack.93.order_ref.refs_0_, bf16[4,560,256]{2,1,0:T(8,128)(2,1)} %fusion.refs_1_, bf16[1024,640]{1,0:T(8,128)(2,1)} %get-tuple-element.118.refs_2_, bf16[1024,1024]{1,0:T(8,128)(2,1)} %get-tuple-element.119.refs_3_.gq_ref, ...), custom_call_target="tpu_custom_call" | custom-call | flops 6000000000 | bytes 18000000 | tf_op jit(solution)/shard_map/attn_gradients_sent/pallas_call | solution.py:911
  241.6 4.9 %collective-permute-done.23 = bf16[4,560,256]{2,1,0:T(8,128)(2,1)S(1)} collective-permute-done((bf16[4,560,256]{2,1,0:T(8,128)(2,1)}, bf16[4,560,256]{2,1,0:T(8,128)(2,1)S(1)}, u32[]{:S(2)}, u32[]{:S(2)}) %collective-permute-start.23) | collective-permute-done | bytes 1146912 | tf_op jit(solution)/shard_map/ppermute | solution.py:462
  246.5 2.1 fusion.2.refs_1_
  249.7 5.7 %attn_gradients_kept.1 = (bf16[2,4,160,192]{3,2,1,0:T(8,128)(2,1)}, bf16[2,4,160,192]{3,2,1,0:T(8,128)(2,1)}) custom-call(s32[12]{0:T(128)} %stack.93.order_ref.refs_0_, bf16[2,560,256]{2,1,0:T(8,128)(2,1)} %fusion.2.refs_1_, bf16[1024,640]{1,0:T(8,128)(2,1)} %get-tuple-element.118.refs_2_, bf16[1024,1024]{1,0:T(8,128)(2,1)} %get-tuple-element.119.refs_3_.gq_ref, ...), custom_call_target="tpu_custom_call" | custom-call | flops 6000000000 | bytes 18000000 | tf_op jit(solution)/shard_map/attn_gradients_kept/pallas_call | solution.py:911
  260.5 5.6 %collective-permute-done.27 = bf16[2,4,160,192]{3,2,1,0:T(8,128)(2,1)S(1)} collective-permute-done((bf16[2,4,160,192]{3,2,1,0:T(8,128)(2,1)}, bf16[2,4,160,192]{3,2,1,0:T(8,128)(2,1)S(1)}, u32[]{:S(2)}, u32[]{:S(2)}) %collective-permute-start.27) | collective-permute-done | bytes 491552 | tf_op jit(solution)/shard_map/ppermute | solution.py:462
  267.9 4.2 %collective-permute-done.24 = bf16[2,560,256]{2,1,0:T(8,128)(2,1)S(1)} collective-permute-done((bf16[2,560,256]{2,1,0:T(8,128)(2,1)}, bf16[2,560,256]{2,1,0:T(8,128)(2,1)S(1)}, u32[]{:S(2)}, u32[]{:S(2)}) %collective-permute-start.24) | collective-permute-done | bytes 573472 | tf_op jit(solution)/shard_map/ppermute | solution.py:462
  275.0 3.4 %collective-permute-start.28 = (bf16[560,256]{1,0:T(8,128)(2,1)}, bf16[560,256]{1,0:T(8,128)(2,1)S(1)}, u32[]{:S(2)}, u32[]{:S(2)}) collective-permute-start(bf16[560,256]{1,0:T(8,128)(2,1)} %fusion.6._), channel_id=1, source_target_pairs={{0,2},{1,3},{2,0},{3,1},{4,6},{5,7},{6,4},{7,5},{8,10},{9,11},{10,... | collective-permute-start | bytes 860168 | tf_op jit(solution)/shard_map/ppermute | solution.py:462
  278.3 7.1 %input_gradient.1 = (bf16[1024,640]{1,0:T(8,128)(2,1)}, f32[8,640]{1,0:T(8,128)}) custom-call(bf16[560,256]{1,0:T(8,128)(2,1)} %fusion.6._, bf16[4,160,192]{2,1,0:T(8,128)(2,1)} %fusion.10.__, bf16[1024,1024]{1,0:T(8,128)(2,1)} %get-tuple-element.119.refs_3_.gq_ref, bf16[1024,512]{1,0:T(8,128)(2,1)} %get-tuple-element.123.refs_4_.gkv_ref, ...), custom_call_target="tpu_custom_call" | custom-call | flops 7000000000 | bytes 21000000 | tf_op jit(solution)/shard_map/input_gradient/pallas_call | solution.py:933
  294.2 3.5 %collective-permute-start.33 = (bf16[160,192]{1,0:T(8,128)(2,1)S(1)}, bf16[160,192]{1,0:T(8,128)(2,1)S(1)}, u32[]{:S(2)}, u32[]{:S(2)}) collective-permute-start(bf16[160,192]{1,0:T(8,128)(2,1)S(1)} %get-tuple-element.148), channel_id=1, source_target_pairs={{0,2},{1,3},{2,0},{3,1},{4,6},{5,7},{6,4},{7,5},{8,10},{9,11},{10,... | collective-permute-start | bytes 184328 | tf_op jit(solution)/shard_map/ppermute | solution.py:462
  300.6 2.1 collective-permute-done.33
  303.9 3.4 %collective-permute-start.39 = (f32[8,640]{1,0:T(8,128)S(1)}, f32[8,640]{1,0:T(8,128)S(1)}, u32[]{:S(2)}, u32[]{:S(2)}) collective-permute-start(f32[8,640]{1,0:T(8,128)S(1)} %add_add_fusion.1), channel_id=1, source_target_pairs={{0,3},{1,2},{2,1},{3,0},{4,7},{5,6},{6,5},{7,4},{8,11},{9,10},{10,... | collective-permute-start | bytes 61448 | tf_op jit(solution)/shard_map/ppermute | solution.py:462
  (168 shorter events, 65.4 us)
Async XLA Ops:
  0.7 23.6 %collective-permute-start.2 = (bf16[2,512,640]{2,1,0:T(8,128)(2,1)}, bf16[2,512,640]{2,1,0:T(8,128)(2,1)S(1)}, u32[]{:S(2)}, u32[]{:S(2)}) collective-permute-start(bf16[2,512,640]{2,1,0:T(8,128)(2,1)} %param.20), channel_id=1, source_target_pairs={{0,4},{4,8},{8,12},{12,16},{16,20},{20,24},{24,28},{1,5},{5,9},{9,... | collective-permute-start | bytes 3932168 | tf_op jit(solution)/shard_map/ppermute | solution.py:457
  6.1 9.2 %collective-permute-start = (bf16[1,160,320]{2,1,0:T(8,128)(2,1)S(1)}, bf16[1,160,320]{2,1,0:T(8,128)(2,1)S(1)}, u32[]{:S(2)}, u32[]{:S(2)}) collective-permute-start(bf16[1,160,320]{2,1,0:T(8,128)(2,1)S(1)} %maximum_bitcast_fusion), channel_id=1, source_target_pairs={{0,2},{1,3},{2,0},{3,1},{4,6},{5,7},{6,4},{7,5},{8,10},{9,11},{10,... | collective-permute-start | bytes 307208 | tf_op jit(solution)/shard_map/ppermute | solution.py:462
  9.6 14.7 %collective-permute-start.3 = (s32[2,512]{1,0:T(2,128)}, s32[2,512]{1,0:T(2,128)S(1)}, u32[]{:S(2)}, u32[]{:S(2)}) collective-permute-start(s32[2,512]{1,0:T(2,128)} %param.21), channel_id=1, source_target_pairs={{0,4},{4,8},{8,12},{12,16},{16,20},{20,24},{24,28},{1,5},{5,9},{9,... | collective-permute-start | bytes 12296 | tf_op jit(solution)/shard_map/ppermute | solution.py:457
  15.4 8.8 %collective-permute-start.1 = (bf16[2,160,320]{2,1,0:T(8,128)(2,1)S(1)}, bf16[2,160,320]{2,1,0:T(8,128)(2,1)S(1)}, u32[]{:S(2)}, u32[]{:S(2)}) collective-permute-start(bf16[2,160,320]{2,1,0:T(8,128)(2,1)S(1)} %pad_maximum_fusion.5), channel_id=1, source_target_pairs={{0,1},{1,0},{2,3},{3,2},{4,5},{5,4},{6,7},{7,6},{8,9},{9,8},{10,11... | collective-permute-start | bytes 614408 | tf_op jit(solution)/shard_map/ppermute | solution.py:462
  24.4 15.3 %collective-permute-start.5 = (bf16[4,160,320]{2,1,0:T(8,128)(2,1)S(1)}, bf16[4,160,320]{2,1,0:T(8,128)(2,1)S(1)}, u32[]{:S(2)}, u32[]{:S(2)}) collective-permute-start(bf16[4,160,320]{2,1,0:T(8,128)(2,1)S(1)} %pad_maximum_fusion.2.refs_0_), channel_id=1, source_target_pairs={{0,16},{4,12},{8,24},{12,4},{16,0},{20,28},{24,8},{28,20},{1,17},{... | collective-permute-start | bytes 1228808 | tf_op jit(solution)/shard_map/ppermute | solution.py:462
  26.7 13.0 %collective-permute-start.4 = (bf16[1,480,256]{2,1,0:T(8,128)(2,1)S(1)}, bf16[1,480,256]{2,1,0:T(8,128)(2,1)S(1)}, u32[]{:S(2)}, u32[]{:S(2)}) collective-permute-start(bf16[1,480,256]{2,1,0:T(8,128)(2,1)S(1)} %bitcast.123), channel_id=1, source_target_pairs={{0,2},{1,3},{2,0},{3,1},{4,6},{5,7},{6,4},{7,5},{8,10},{9,11},{10,... | collective-permute-start | bytes 737288 | tf_op jit(solution)/shard_map/ppermute | solution.py:462
  40.5 12.3 %collective-permute-start.8 = (bf16[2,480,256]{2,1,0:T(8,128)(2,1)S(1)}, bf16[2,480,256]{2,1,0:T(8,128)(2,1)S(1)}, u32[]{:S(2)}, u32[]{:S(2)}) collective-permute-start(bf16[2,480,256]{2,1,0:T(8,128)(2,1)S(1)} %pad_maximum_fusion.3), channel_id=1, source_target_pairs={{0,1},{1,0},{2,3},{3,2},{4,5},{5,4},{6,7},{7,6},{8,9},{9,8},{10,11... | collective-permute-start | bytes 1474568 | tf_op jit(solution)/shard_map/ppermute | solution.py:462
  41.8 8.9 %collective-permute-start.6 = (bf16[4,160,320]{2,1,0:T(8,128)(2,1)S(1)}, bf16[4,160,320]{2,1,0:T(8,128)(2,1)}, u32[]{:S(2)}, u32[]{:S(2)}) collective-permute-start(bf16[4,160,320]{2,1,0:T(8,128)(2,1)S(1)} %pad_maximum_fusion.2.refs_0_), channel_id=1, source_target_pairs={{0,8},{4,20},{8,0},{12,28},{16,24},{20,4},{24,16},{28,12},{1,9},{5... | collective-permute-start | bytes 1228808 | tf_op jit(solution)/shard_map/ppermute | solution.py:462
  42.8 14.8 %collective-permute-start.9 = (bf16[4,160,320]{2,1,0:T(8,128)(2,1)S(1)}, bf16[4,160,320]{2,1,0:T(8,128)(2,1)}, u32[]{:S(2)}, u32[]{:S(2)}) collective-permute-start(bf16[4,160,320]{2,1,0:T(8,128)(2,1)S(1)} %pad_maximum_fusion.2.refs_0_), channel_id=1, source_target_pairs={{0,4},{4,0},{8,12},{12,8},{16,20},{20,16},{24,28},{28,24},{1,5},{5... | collective-permute-start | bytes 1228808 | tf_op jit(solution)/shard_map/ppermute | solution.py:462
  42.8 13.2 %collective-permute-start.7 = (bf16[4,160,320]{2,1,0:T(8,128)(2,1)}, bf16[4,160,320]{2,1,0:T(8,128)(2,1)}, u32[]{:S(2)}, u32[]{:S(2)}) collective-permute-start(bf16[4,160,320]{2,1,0:T(8,128)(2,1)} %copy-done.18), channel_id=1, source_target_pairs={{0,8},{4,20},{8,0},{12,28},{16,24},{20,4},{24,16},{28,12},{1,9},{5... | collective-permute-start | bytes 1228808 | tf_op jit(solution)/shard_map/ppermute | solution.py:462
  45.5 12.3 %collective-permute-start.10 = (bf16[4,160,320]{2,1,0:T(8,128)(2,1)}, bf16[4,160,320]{2,1,0:T(8,128)(2,1)}, u32[]{:S(2)}, u32[]{:S(2)}) collective-permute-start(bf16[4,160,320]{2,1,0:T(8,128)(2,1)} %copy-done.18), channel_id=1, source_target_pairs={{0,4},{4,0},{8,12},{12,8},{16,20},{20,16},{24,28},{28,24},{1,5},{5... | collective-permute-start | bytes 1228808 | tf_op jit(solution)/shard_map/ppermute | solution.py:462
  50.7 7.1 %collective-permute-start.11 = (bf16[4,160,320]{2,1,0:T(8,128)(2,1)}, bf16[4,160,320]{2,1,0:T(8,128)(2,1)}, u32[]{:S(2)}, u32[]{:S(2)}) collective-permute-start(bf16[4,160,320]{2,1,0:T(8,128)(2,1)} %collective-permute-done.6.refs_2_), channel_id=1, source_target_pairs={{0,4},{4,0},{8,12},{12,8},{16,20},{20,16},{24,28},{28,24},{1,5},{5... | collective-permute-start | bytes 1228808 | tf_op jit(solution)/shard_map/ppermute | solution.py:462
  57.1 14.2 %collective-permute-start.13 = (bf16[4,480,256]{2,1,0:T(8,128)(2,1)S(1)}, bf16[4,480,256]{2,1,0:T(8,128)(2,1)}, u32[]{:S(2)}, u32[]{:S(2)}) collective-permute-start(bf16[4,480,256]{2,1,0:T(8,128)(2,1)S(1)} %pad_maximum_fusion.1.refs_0_), channel_id=1, source_target_pairs={{0,16},{4,12},{8,24},{12,4},{16,0},{20,28},{24,8},{28,20},{1,17},{... | collective-permute-start | bytes 2949128 | tf_op jit(solution)/shard_map/ppermute | solution.py:462
  57.6 39.8 %collective-permute-start.16 = (bf16[4,480,256]{2,1,0:T(8,128)(2,1)S(1)}, bf16[4,480,256]{2,1,0:T(8,128)(2,1)}, u32[]{:S(2)}, u32[]{:S(2)}) collective-permute-start(bf16[4,480,256]{2,1,0:T(8,128)(2,1)S(1)} %pad_maximum_fusion.1.refs_0_), channel_id=1, source_target_pairs={{0,4},{4,0},{8,12},{12,8},{16,20},{20,16},{24,28},{28,24},{1,5},{5... | collective-permute-start | bytes 2949128 | tf_op jit(solution)/shard_map/ppermute | solution.py:462
  71.3 24.9 %collective-permute-start.15 = (bf16[4,480,256]{2,1,0:T(8,128)(2,1)}, bf16[4,480,256]{2,1,0:T(8,128)(2,1)S(1)}, u32[]{:S(2)}, u32[]{:S(2)}) collective-permute-start(bf16[4,480,256]{2,1,0:T(8,128)(2,1)} %collective-permute-done.13.refs_1_), channel_id=1, source_target_pairs={{0,8},{4,20},{8,0},{12,28},{16,24},{20,4},{24,16},{28,12},{1,9},{5... | collective-permute-start | bytes 2949128 | tf_op jit(solution)/shard_map/ppermute | solution.py:462
  71.8 25.7 %collective-permute-start.17 = (bf16[4,480,256]{2,1,0:T(8,128)(2,1)}, bf16[4,480,256]{2,1,0:T(8,128)(2,1)}, u32[]{:S(2)}, u32[]{:S(2)}) collective-permute-start(bf16[4,480,256]{2,1,0:T(8,128)(2,1)} %collective-permute-done.13.refs_1_), channel_id=1, source_target_pairs={{0,4},{4,0},{8,12},{12,8},{16,20},{20,16},{24,28},{28,24},{1,5},{5... | collective-permute-start | bytes 2949128 | tf_op jit(solution)/shard_map/ppermute | solution.py:462
  71.8 24.5 %collective-permute-start.14 = (bf16[4,480,256]{2,1,0:T(8,128)(2,1)S(1)}, bf16[4,480,256]{2,1,0:T(8,128)(2,1)}, u32[]{:S(2)}, u32[]{:S(2)}) collective-permute-start(bf16[4,480,256]{2,1,0:T(8,128)(2,1)S(1)} %pad_maximum_fusion.1.refs_0_), channel_id=1, source_target_pairs={{0,8},{4,20},{8,0},{12,28},{16,24},{20,4},{24,16},{28,12},{1,9},{5... | collective-permute-start | bytes 2949128 | tf_op jit(solution)/shard_map/ppermute | solution.py:462
  164.5 17.0 %collective-permute-start.20 = (bf16[4,4,320,256]{3,2,1,0:T(8,128)(2,1)}, bf16[4,4,320,256]{3,2,1,0:T(8,128)(2,1)S(1)}, u32[]{:S(2)}, u32[]{:S(2)}) collective-permute-start(bf16[4,4,320,256]{3,2,1,0:T(8,128)(2,1)} %get-tuple-element.109), channel_id=1, source_target_pairs={{0,4},{4,0},{8,12},{12,8},{16,20},{20,16},{24,28},{28,24},{1,5},{5... | collective-permute-start | bytes 7864328 | tf_op jit(solution)/shard_map/ppermute | solution.py:462
  164.7 16.8 %collective-permute-start.21 = (bf16[4,4,240,256]{3,2,1,0:T(8,128)(2,1)}, bf16[4,4,240,256]{3,2,1,0:T(8,128)(2,1)}, u32[]{:S(2)}, u32[]{:S(2)}) collective-permute-start(bf16[4,4,240,256]{3,2,1,0:T(8,128)(2,1)} %get-tuple-element.110), channel_id=1, source_target_pairs={{0,4},{4,0},{8,12},{12,8},{16,20},{20,16},{24,28},{28,24},{1,5},{5... | collective-permute-start | bytes 5898248 | tf_op jit(solution)/shard_map/ppermute | solution.py:462
  187.0 28.5 %collective-permute-start.22 = (bf16[2,4,560,256]{3,2,1,0:T(8,128)(2,1)}, bf16[2,4,560,256]{3,2,1,0:T(8,128)(2,1)}, u32[]{:S(2)}, u32[]{:S(2)}) collective-permute-start(bf16[2,4,560,256]{3,2,1,0:T(8,128)(2,1)} %pad_maximum_fusion._), channel_id=1, source_target_pairs={{0,8},{4,20},{8,0},{12,28},{16,24},{20,4},{24,16},{28,12},{1,9},{5... | collective-permute-start | bytes 6881288 | tf_op jit(solution)/shard_map/ppermute | solution.py:462
  218.0 28.6 %collective-permute-start.23 = (bf16[4,560,256]{2,1,0:T(8,128)(2,1)}, bf16[4,560,256]{2,1,0:T(8,128)(2,1)S(1)}, u32[]{:S(2)}, u32[]{:S(2)}) collective-permute-start(bf16[4,560,256]{2,1,0:T(8,128)(2,1)} %fusion.refs_1_), channel_id=1, source_target_pairs={{0,16},{4,12},{8,24},{12,4},{16,0},{20,28},{24,8},{28,20},{1,17},{... | collective-permute-start | bytes 3440648 | tf_op jit(solution)/shard_map/ppermute | solution.py:462
  238.0 10.6 %collective-permute-start.26 = (bf16[4,4,160,192]{3,2,1,0:T(8,128)(2,1)}, bf16[4,4,160,192]{3,2,1,0:T(8,128)(2,1)S(1)}, u32[]{:S(2)}, u32[]{:S(2)}) collective-permute-start(bf16[4,4,160,192]{3,2,1,0:T(8,128)(2,1)} %attn_gradients_sent.1), channel_id=1, source_target_pairs={{0,4},{4,0},{8,12},{12,8},{16,20},{20,16},{24,28},{28,24},{1,5},{5... | collective-permute-start | bytes 2949128 | tf_op jit(solution)/shard_map/ppermute | solution.py:462
  255.3 10.8 %collective-permute-start.27 = (bf16[2,4,160,192]{3,2,1,0:T(8,128)(2,1)}, bf16[2,4,160,192]{3,2,1,0:T(8,128)(2,1)S(1)}, u32[]{:S(2)}, u32[]{:S(2)}) collective-permute-start(bf16[2,4,160,192]{3,2,1,0:T(8,128)(2,1)} %get-tuple-element.125), channel_id=1, source_target_pairs={{0,8},{4,20},{8,0},{12,28},{16,24},{20,4},{24,16},{28,12},{1,9},{5... | collective-permute-start | bytes 1474568 | tf_op jit(solution)/shard_map/ppermute | solution.py:462
  257.2 14.9 %collective-permute-start.24 = (bf16[2,560,256]{2,1,0:T(8,128)(2,1)}, bf16[2,560,256]{2,1,0:T(8,128)(2,1)S(1)}, u32[]{:S(2)}, u32[]{:S(2)}) collective-permute-start(bf16[2,560,256]{2,1,0:T(8,128)(2,1)} %fusion.2.refs_1_), channel_id=1, source_target_pairs={{0,1},{1,0},{2,3},{3,2},{4,5},{5,4},{6,7},{7,6},{8,9},{9,8},{10,11... | collective-permute-start | bytes 1720328 | tf_op jit(solution)/shard_map/ppermute | solution.py:462
  273.8 13.7 %collective-permute-start.29 = (bf16[4,160,192]{2,1,0:T(8,128)(2,1)}, bf16[4,160,192]{2,1,0:T(8,128)(2,1)}, u32[]{:S(2)}, u32[]{:S(2)}) collective-permute-start(bf16[4,160,192]{2,1,0:T(8,128)(2,1)} %fusion.10.__), channel_id=1, source_target_pairs={{0,16},{4,12},{8,24},{12,4},{16,0},{20,28},{24,8},{28,20},{1,17},{... | collective-permute-start | bytes 737288 | tf_op jit(solution)/shard_map/ppermute | solution.py:462
  275.0 22.8 %collective-permute-start.28 = (bf16[560,256]{1,0:T(8,128)(2,1)}, bf16[560,256]{1,0:T(8,128)(2,1)S(1)}, u32[]{:S(2)}, u32[]{:S(2)}) collective-permute-start(bf16[560,256]{1,0:T(8,128)(2,1)} %fusion.6._), channel_id=1, source_target_pairs={{0,2},{1,3},{2,0},{3,1},{4,6},{5,7},{6,4},{7,5},{8,10},{9,11},{10,... | collective-permute-start | bytes 860168 | tf_op jit(solution)/shard_map/ppermute | solution.py:462
  290.7 7.0 %collective-permute-start.36 = (f32[8,640]{1,0:T(8,128)S(1)}, f32[8,640]{1,0:T(8,128)S(1)}, u32[]{:S(2)}, u32[]{:S(2)}) collective-permute-start(f32[8,640]{1,0:T(8,128)S(1)} %add.257), channel_id=1, source_target_pairs={{0,24},{4,28},{8,16},{12,20},{16,8},{20,12},{24,0},{28,4},{1,25},{... | collective-permute-start | bytes 61448 | tf_op jit(solution)/shard_map/ppermute | solution.py:462
  293.3 7.3 %collective-permute-start.31 = (bf16[160,192]{1,0:T(8,128)(2,1)S(1)}, bf16[160,192]{1,0:T(8,128)(2,1)S(1)}, u32[]{:S(2)}, u32[]{:S(2)}) collective-permute-start(bf16[160,192]{1,0:T(8,128)(2,1)S(1)} %get-tuple-element.146), channel_id=1, source_target_pairs={{0,3},{1,2},{2,1},{3,0},{4,7},{5,6},{6,5},{7,4},{8,11},{9,10},{10,... | collective-permute-start | bytes 184328 | tf_op jit(solution)/shard_map/ppermute | solution.py:462
  294.2 8.5 %collective-permute-start.33 = (bf16[160,192]{1,0:T(8,128)(2,1)S(1)}, bf16[160,192]{1,0:T(8,128)(2,1)S(1)}, u32[]{:S(2)}, u32[]{:S(2)}) collective-permute-start(bf16[160,192]{1,0:T(8,128)(2,1)S(1)} %get-tuple-element.148), channel_id=1, source_target_pairs={{0,2},{1,3},{2,0},{3,1},{4,6},{5,7},{6,4},{7,5},{8,10},{9,11},{10,... | collective-permute-start | bytes 184328 | tf_op jit(solution)/shard_map/ppermute | solution.py:462
  302.8 8.6 %collective-permute-start.37 = (f32[8,640]{1,0:T(8,128)S(1)}, f32[8,640]{1,0:T(8,128)S(1)}, u32[]{:S(2)}, u32[]{:S(2)}) collective-permute-start(f32[8,640]{1,0:T(8,128)S(1)} %add_add_fusion.1), channel_id=1, source_target_pairs={{0,1},{1,0},{2,3},{3,2},{4,5},{5,4},{6,7},{7,6},{8,9},{9,8},{10,11... | collective-permute-start | bytes 61448 | tf_op jit(solution)/shard_map/ppermute | solution.py:462
  303.1 8.3 %collective-permute-start.38 = (f32[8,640]{1,0:T(8,128)S(1)}, f32[8,640]{1,0:T(8,128)S(1)}, u32[]{:S(2)}, u32[]{:S(2)}) collective-permute-start(f32[8,640]{1,0:T(8,128)S(1)} %add_add_fusion.1), channel_id=1, source_target_pairs={{0,2},{1,3},{2,0},{3,1},{4,6},{5,7},{6,4},{7,5},{8,10},{9,11},{10,... | collective-permute-start | bytes 61448 | tf_op jit(solution)/shard_map/ppermute | solution.py:462
  303.9 7.6 %collective-permute-start.39 = (f32[8,640]{1,0:T(8,128)S(1)}, f32[8,640]{1,0:T(8,128)S(1)}, u32[]{:S(2)}, u32[]{:S(2)}) collective-permute-start(f32[8,640]{1,0:T(8,128)S(1)} %add_add_fusion.1), channel_id=1, source_target_pairs={{0,3},{1,2},{2,1},{3,0},{4,7},{5,6},{6,5},{7,4},{8,11},{9,10},{10,... | collective-permute-start | bytes 61448 | tf_op jit(solution)/shard_map/ppermute | solution.py:462
  (28 other events, 378.2 us)
where the time goes:
time: 314 us; the launch traced here: 313 us
  Pallas kernels  126 us (40%)
  waiting for transfers between devices  81.9 us (26%)
  starting transfers between devices  60.6 us (19%)
  other arithmetic  27.2 us (9%)
  local copies, waits for them, and re-layouts  16.3 us (5%)
    ppermute x37, waiting for transfers between devices, swapped(): lax.ppermute(array, axis, [(i, i ^ (odd if i % 2 else even)) for i in ran...  81.8 us
    pallas_call x1, Pallas kernels, body(): pl.pallas_call(ffn_kernel, grid=(tiles + pieces,), in_specs=[smem, smem,...  64.1 us
    ppermute x37, starting transfers between devices, swapped(): lax.ppermute(array, axis, [(i, i ^ (odd if i % 2 else even)) for i in ran...  53.5 us
    pallas_call x1, Pallas kernels, body(): pl.pallas_call(attn_back_kernel, grid=(seq_dev,), in_specs=[rows(block, i...  16.4 us
    pallas_call x1, Pallas kernels, body(): pl.pallas_call(attn_kernel, grid=(seq_dev,), in_specs=[rows(block, inner)...  12.1 us
    pallas_call x2, Pallas kernels, attn_parts(): pl.pallas_call(lambda *refs: attn_grad_kernel(base, *refs), in_specs=[sme...  11.1 us
    pallas_call x1, Pallas kernels, body(): pl.pallas_call(qkv_kernel, grid=(seq_dev,), in_specs=[smem, tok_spec, tok...  11 us
    add x11, other arithmetic, total(): result = result + term.astype(f32)  10.9 us
  transfers between devices with their start and end apart: 40, of which 20 were waited for; matrix products, arithmetic and copies ran while one was open for 9% of the time, Pallas kernels for 18%

commit v1 on v0

--- a/solution.py
+++ b/solution.py
@@ -359,7 +359,7 @@
 
 
 def attn_back_kernel(
-    q_ref, gctx_ref, key_ref, val_ref, pos_ref, lse_ref, qraw_ref, cos_ref, sin_ref, head_ref,
+    _, q_ref, gctx_ref, key_ref, val_ref, pos_ref, lse_ref, qraw_ref, cos_ref, sin_ref, head_ref,
     gq_ref, far_ref, near_ref, gain_ref, gkey_ref, gval_ref,
 ):
     head_dim = key_ref.shape[2]
@@ -852,11 +852,16 @@
         gate_got, down_got = swapped(gate_sent, "seq", 1, 1), swapped(down_sent, "seq", 1, 1)
 
 
+    ffn = ffn_parts
+    if exchange.direct:
+        kept, got = (gate_kept, down_kept), (gate_got, down_got)
+        ffn = exchange.split([(kept, 0), (got, 0)], 0)
+
     pair = pl.BlockSpec((1, block, 2 * head_dim), lambda i: (i, 0, 0))
     g_query, g_far, g_near, query_gain = pl.pallas_call(
         attn_back_kernel,
         grid=(seq_dev,),
-        in_specs=[rows(block, inner), rows(block, inner), key_spec, key_spec]
+        in_specs=[remain, rows(block, inner), rows(block, inner), key_spec, key_spec]
         + [rows(block, 1), rows(block, 128), rows(block, inner), table_spec, table_spec]
         + [head_spec],
         out_specs=[rows(block, inner), pair, pair, whole((8, head_dim))],
@@ -874,15 +879,13 @@
         name="attention_gradient",
         cost_estimate=cost(16),
     )(
-        query_rot, g_ctx, keys, values, pos_column, log_total, query_raw, cosine, sine,
+        ffn[0], query_rot, g_ctx, keys, values, pos_column, log_total, query_raw, cosine, sine,
         head_gains,
     )
     g_recv = passed_along(g_far, "seq", -1)
-    ffn = ffn_parts
+    early = ffn
     if exchange.direct:
-        gate_got, down_got, g_query = lax.optimization_barrier((gate_got, down_got, g_query))
-        kept, got = (gate_kept, down_kept), (gate_got, down_got)
-        ffn = exchange.split([(kept, 0), (got, 0)], 0)
+        ffn = early = exchange.fold(*ffn, 1)
     g_kv, key_gain = pl.pallas_call(
         kv_back_kernel,
         grid=(seq_dev,),
@@ -893,7 +896,7 @@
         compiler_params=params(),
         name="key_value_back",
         cost_estimate=cost(4),
-    )(key_raw, own_cosine, own_sine, head_gains, g_near, g_recv, ffn[0])
+    )(key_raw, own_cosine, own_sine, head_gains, g_near, g_recv, early[0])
 
     each = head_dim // pieces
     column = jnp.arange(2 * head_dim, dtype=jnp.int32)
@@ -919,9 +922,6 @@
             name="attn_gradients_kept" if base else "attn_gradients_sent",
         )(exchange.order, before, attn_low, g_query, g_kv, chosen, *extra)
 
-    early = ffn
-    if exchange.direct:
-        ffn = early = exchange.fold(*ffn, 1)
     (attn_sent,) = attn_parts(0, early[0], [])
     attn_got = exchange.swap_cores(attn_sent) if exchange.direct else jnp.zeros_like(attn_sent)
     if exchange.direct:

time: 314 us -> 299 us (0.952)
  waiting for transfers between devices: 81.9 us -> 69.4 us
  local copies, waits for them, and re-layouts: 16.3 us -> 12.4 us
    ppermute x37, waiting for transfers between devices: 81.8 us -> 69.4 us  [swapped(): lax.ppermute(array, axis, [(i, i ^ (odd if i % 2 else even)) for i in ran...]
    unnamed x47 -> x45, local copies, waits for them, and re-layouts: 7.5 us -> 3.53 us
  transfers between devices with their start and end apart: 40 -> 40, of which waited for: 20 -> 20; matrix products, arithmetic and copies ran while one was open for 9% -> 11% of each run, Pallas kernels for 18% -> 19%
where the time goes in v1:
time: 299 us; the launch traced here: 298 us
  Pallas kernels  125 us (42%)
  waiting for transfers between devices  69.4 us (23%)
  starting transfers between devices  61.8 us (21%)
  other arithmetic  28.1 us (9%)
  local copies, waits for them, and re-layouts  12.4 us (4%)
    ppermute x37, waiting for transfers between devices, swapped(): lax.ppermute(array, axis, [(i, i ^ (odd if i % 2 else even)) for i in ran...  69.4 us
    pallas_call x1, Pallas kernels, body(): pl.pallas_call(ffn_kernel, grid=(tiles + pieces,), in_specs=[smem, smem,...  64.1 us
    ppermute x37, starting transfers between devices, swapped(): lax.ppermute(array, axis, [(i, i ^ (odd if i % 2 else even)) for i in ran...  54.6 us
    pallas_call x1, Pallas kernels, body(): pl.pallas_call(attn_back_kernel, grid=(seq_dev,), in_specs=[remain, rows(...  16.3 us
    pallas_call x1, Pallas kernels, body(): pl.pallas_call(attn_kernel, grid=(seq_dev,), in_specs=[rows(block, inner)...  12.1 us
    add x11, other arithmetic, total(): result = result + term.astype(f32)  11.2 us
    pallas_call x2, Pallas kernels, attn_parts(): pl.pallas_call(lambda *refs: attn_grad_kernel(base, *refs), in_specs=[sme...  11.1 us
    pallas_call x1, Pallas kernels, body(): pl.pallas_call(qkv_kernel, grid=(seq_dev,), in_specs=[smem, tok_spec, tok...  11 us
  transfers between devices with their start and end apart: 40, of which 20 were waited for; matrix products, arithmetic and copies ran while one was open for 11% of the time, Pallas kernels for 19%

profile of v1, /device:TPU:0, one launch (start us, length us, event | category | flops | bytes accessed | tf_op | source)
XLA Modules:
  0.0 298.4 jit_solution(7237752533181923558)
XLA Ops:
  0.7 2.6 collective-permute-start.2
  6.1 3.5 %collective-permute-start = (bf16[1,160,320]{2,1,0:T(8,128)(2,1)S(1)}, bf16[1,160,320]{2,1,0:T(8,128)(2,1)S(1)}, u32[]{:S(2)}, u32[]{:S(2)}) collective-permute-start(bf16[1,160,320]{2,1,0:T(8,128)(2,1)S(1)} %maximum_bitcast_fusion), channel_id=1, source_target_pairs={{0,2},{1,3},{2,0},{3,1},{4,6},{5,7},{6,4},{7,5},{8,10},{9,11},{10,... | collective-permute-start | bytes 307208 | tf_op jit(solution)/shard_map/ppermute | solution.py:462
  9.6 3.3 %collective-permute-start.3 = (s32[2,512]{1,0:T(2,128)}, s32[2,512]{1,0:T(2,128)S(1)}, u32[]{:S(2)}, u32[]{:S(2)}) collective-permute-start(s32[2,512]{1,0:T(2,128)} %param.21), channel_id=1, source_target_pairs={{0,4},{4,8},{8,12},{12,16},{16,20},{20,24},{24,28},{1,5},{5,9},{9,... | collective-permute-start | bytes 12296 | tf_op jit(solution)/shard_map/ppermute | solution.py:457
  13.2 2.2 collective-permute-done
  15.4 2.1 collective-permute-start.1
  18.4 5.8 %collective-permute-done.1 = bf16[2,160,320]{2,1,0:T(8,128)(2,1)S(1)} collective-permute-done((bf16[2,160,320]{2,1,0:T(8,128)(2,1)S(1)}, bf16[2,160,320]{2,1,0:T(8,128)(2,1)S(1)}, u32[]{:S(2)}, u32[]{:S(2)}) %collective-permute-start.1) | collective-permute-done | bytes 204832 | tf_op jit(solution)/shard_map/ppermute | solution.py:462
  24.4 2.3 collective-permute-start.5
  26.7 2.3 collective-permute-start.4
  29.7 10.0 %collective-permute-done.4 = bf16[1,480,256]{2,1,0:T(8,128)(2,1)S(1)} collective-permute-done((bf16[1,480,256]{2,1,0:T(8,128)(2,1)S(1)}, bf16[1,480,256]{2,1,0:T(8,128)(2,1)S(1)}, u32[]{:S(2)}, u32[]{:S(2)}) %collective-permute-start.4) | collective-permute-done | bytes 245792 | tf_op jit(solution)/shard_map/ppermute | solution.py:462
  45.2 4.9 %collective-permute-done.6.refs_2_ = bf16[4,160,320]{2,1,0:T(8,128)(2,1)} collective-permute-done((bf16[4,160,320]{2,1,0:T(8,128)(2,1)S(1)}, bf16[4,160,320]{2,1,0:T(8,128)(2,1)}, u32[]{:S(2)}, u32[]{:S(2)}) %collective-permute-start.6) | collective-permute-done | bytes 409632 | tf_op jit(solution)/shard_map/ppermute | solution.py:462
  50.1 2.0 collective-permute-done.8
  52.2 3.2 %collective-permute-done.7.refs_3_ = bf16[4,160,320]{2,1,0:T(8,128)(2,1)} collective-permute-done((bf16[4,160,320]{2,1,0:T(8,128)(2,1)S(1)}, bf16[4,160,320]{2,1,0:T(8,128)(2,1)}, u32[]{:S(2)}, u32[]{:S(2)}) %collective-permute-start.7) | collective-permute-done | bytes 409632 | tf_op jit(solution)/shard_map/ppermute | solution.py:462
  57.6 11.0 %project_rotate.1 = (bf16[1024,640]{1,0:T(8,128)(2,1)}, f32[1024,1024]{1,0:T(8,128)}, bf16[1024,1024]{1,0:T(8,128)(2,1)}, f32[1024,256]{1,0:T(8,128)}, bf16[2,10...) custom-call(s32[12]{0:T(128)} %stack.92.held_ref, ...), custom_call_target="tpu_custom_call" | custom-call | flops 11000000512 | bytes 33000000 | tf_op jit(solution)/shard_map/project_rotate/pallas_call | solution.py:729
  68.5 2.1 collective-permute-done.13.refs_1_
  72.6 12.1 %window_attention.1 = (bf16[1024,1024]{1,0:T(8,128)(2,1)}, f32[1024,128]{1,0:T(8,128)}, f32[1024,640]{1,0:T(8,128)}, f32[1024,640]{1,0:T(8,128)}, bf16[1024,640]{1,0:T(8,128)(2,1)}) custom-call(bf16[1024,1024]{1,0:T(8,128)(2,1)} %get-tuple-element.88.q_ref, bf16[2,1024,256]{2,1,0:T(8,128)(2,1)} %get-tuple-element.91.key_ref, ...), custom_call_target="tpu_custom_call" | custom-call | flops 12000000000 | bytes 36000000 | tf_op jit(solution)/shard_map/window_attention/pallas_call | solution.py:770
  84.7 10.6 %collective-permute-done.14.refs_2_ = bf16[4,480,256]{2,1,0:T(8,128)(2,1)} collective-permute-done((bf16[4,480,256]{2,1,0:T(8,128)(2,1)S(1)}, bf16[4,480,256]{2,1,0:T(8,128)(2,1)}, u32[]{:S(2)}, u32[]{:S(2)}) %collective-permute-start.14) | collective-permute-done | bytes 983072 | tf_op jit(solution)/shard_map/ppermute | solution.py:462
  99.6 64.1 %feed_forward.1 = (bf16[1024,640]{1,0:T(8,128)(2,1)}, f32[1024,640]{1,0:T(8,128)}, bf16[1024,1024]{1,0:T(8,128)(2,1)}, f32[8,640]{1,0:T(8,128)}, bf16[4,4,320,25...) custom-call(s32[12]{0:T(128)} %stack.92.held_ref, ...), custom_call_target="tpu_custom_call" | custom-call | flops 60000002048 | bytes 180000000 | tf_op jit(solution)/shard_map/feed_forward/pallas_call | solution.py:820
  164.7 7.2 %collective-permute-done.21 = bf16[4,4,240,256]{3,2,1,0:T(8,128)(2,1)} collective-permute-done((bf16[4,4,240,256]{3,2,1,0:T(8,128)(2,1)}, bf16[4,4,240,256]{3,2,1,0:T(8,128)(2,1)}, u32[]{:S(2)}, u32[]{:S(2)}) %collective-permute-start.21) | collective-permute-done | bytes 1966112 | tf_op jit(solution)/shard_map/ppermute | solution.py:462
  177.2 16.3 %attention_gradient.1 = (bf16[1024,1024]{1,0:T(8,128)(2,1)}, bf16[2,512,512]{2,1,0:T(8,128)(2,1)}, f32[2,512,512]{2,1,0:T(8,128)}, f32[8,256]{1,0:T(8,128)}) custom-call(bf16[2,4,560,256]{3,2,1,0:T(8,128)(2,1)} %pad_maximum_fusion._, bf16[1024,1024]{1,0:T(8,128)(2,1)} %get-tuple-element.88.q_ref, bf16[1024,1024]{1,0:T(8,128)(2,1)} %get-tuple-element.110.gctx_ref, ...), custom_call_target="tpu_custom_call" | custom-call | flops 16000000000 | bytes 48000000 | tf_op jit(solution)/shard_map/attention_gradient/pallas_call | solution.py:861
  198.2 7.0 %collective-permute-done.22 = bf16[2,4,560,256]{3,2,1,0:T(8,128)(2,1)S(1)} collective-permute-done((bf16[2,4,560,256]{3,2,1,0:T(8,128)(2,1)}, bf16[2,4,560,256]{3,2,1,0:T(8,128)(2,1)S(1)}, u32[]{:S(2)}, u32[]{:S(2)}) %collective-permute-start.22) | collective-permute-done | bytes 2293792 | tf_op jit(solution)/shard_map/ppermute | solution.py:462
  207.0 3.9 %key_value_back.1 = (bf16[1024,512]{1,0:T(8,128)(2,1)}, f32[8,256]{1,0:T(8,128)}) custom-call(f32[1024,256]{1,0:T(8,128)} %get-tuple-element.114.kraw_ref, f32[512,128]{1,0:T(8,128)} %constant.82.clone.cos_ref, f32[512,128]{1,0:T(8,128)} %constant.83.clone.sin_ref, f32[2,256]{1,0:T(2,128)} %pad_maximum_fusion.8.head_ref, ...), custom_call_target="tpu_custom_call" | custom-call | flops 4000000000 | bytes 12000000 | tf_op jit(solution)/shard_map/key_value_back/pallas_call | solution.py:889
  210.9 5.4 %attn_gradients_sent.1 = bf16[4,4,160,192]{3,2,1,0:T(8,128)(2,1)} custom-call(s32[12]{0:T(128)} %stack.93.order_ref.refs_0_, bf16[4,560,256]{2,1,0:T(8,128)(2,1)} %fusion._.refs_1_, bf16[1024,640]{1,0:T(8,128)(2,1)} %get-tuple-element.109.refs_2_, bf16[1024,1024]{1,0:T(8,128)(2,1)} %get-tuple-element.113.refs_3_.gq_ref, ...), custom_call_target="tpu_custom_call" | custom-call | flops 6000000000 | bytes 18000000 | tf_op jit(solution)/shard_map/attn_gradients_sent/pallas_call | solution.py:914
  216.3 16.8 %collective-permute-start.26 = (bf16[4,4,160,192]{3,2,1,0:T(8,128)(2,1)}, bf16[4,4,160,192]{3,2,1,0:T(8,128)(2,1)}, u32[]{:S(2)}, u32[]{:S(2)}) collective-permute-start(bf16[4,4,160,192]{3,2,1,0:T(8,128)(2,1)} %attn_gradients_sent.1), channel_id=1, source_target_pairs={{0,4},{4,0},{8,12},{12,8},{16,20},{20,16},{24,28},{28,24},{1,5},{5... | collective-permute-start | bytes 2949128 | tf_op jit(solution)/shard_map/ppermute | solution.py:462
  235.2 2.1 fusion.2.refs_1_
  237.3 5.7 %attn_gradients_kept.1 = (bf16[2,4,160,192]{3,2,1,0:T(8,128)(2,1)}, bf16[2,4,160,192]{3,2,1,0:T(8,128)(2,1)}) custom-call(s32[12]{0:T(128)} %stack.93.order_ref.refs_0_, bf16[2,560,256]{2,1,0:T(8,128)(2,1)} %fusion.2.refs_1_, bf16[1024,640]{1,0:T(8,128)(2,1)} %get-tuple-element.109.refs_2_, bf16[1024,1024]{1,0:T(8,128)(2,1)} %get-tuple-element.113.refs_3_.gq_ref, ...), custom_call_target="tpu_custom_call" | custom-call | flops 6000000000 | bytes 18000000 | tf_op jit(solution)/shard_map/attn_gradients_kept/pallas_call | solution.py:914
  248.3 5.5 %collective-permute-done.27 = bf16[2,4,160,192]{3,2,1,0:T(8,128)(2,1)S(1)} collective-permute-done((bf16[2,4,160,192]{3,2,1,0:T(8,128)(2,1)}, bf16[2,4,160,192]{3,2,1,0:T(8,128)(2,1)S(1)}, u32[]{:S(2)}, u32[]{:S(2)}) %collective-permute-start.27) | collective-permute-done | bytes 491552 | tf_op jit(solution)/shard_map/ppermute | solution.py:462
  256.4 2.0 collective-permute-done.24
  258.4 2.0 fusion.6._
  261.2 3.4 %collective-permute-start.28 = (bf16[560,256]{1,0:T(8,128)(2,1)}, bf16[560,256]{1,0:T(8,128)(2,1)}, u32[]{:S(2)}, u32[]{:S(2)}) collective-permute-start(bf16[560,256]{1,0:T(8,128)(2,1)} %fusion.6._), channel_id=1, source_target_pairs={{0,2},{1,3},{2,0},{3,1},{4,6},{5,7},{6,4},{7,5},{8,10},{9,11},{10,... | collective-permute-start | bytes 860168 | tf_op jit(solution)/shard_map/ppermute | solution.py:462
  264.7 7.1 %input_gradient.1 = (bf16[1024,640]{1,0:T(8,128)(2,1)}, f32[8,640]{1,0:T(8,128)}) custom-call(bf16[560,256]{1,0:T(8,128)(2,1)} %fusion.6._, bf16[4,160,192]{2,1,0:T(8,128)(2,1)} %fusion.10.__, bf16[1024,1024]{1,0:T(8,128)(2,1)} %get-tuple-element.113.refs_3_.gq_ref, bf16[1024,512]{1,0:T(8,128)(2,1)} %get-tuple-element.117.refs_4_.gkv_ref, ...), custom_call_target="tpu_custom_call" | custom-call | flops 7000000000 | bytes 21000000 | tf_op jit(solution)/shard_map/input_gradient/pallas_call | solution.py:933
  275.2 2.2 collective-permute-start.34
  281.2 3.2 %collective-permute-start.33 = (bf16[160,192]{1,0:T(8,128)(2,1)S(1)}, bf16[160,192]{1,0:T(8,128)(2,1)S(1)}, u32[]{:S(2)}, u32[]{:S(2)}) collective-permute-start(bf16[160,192]{1,0:T(8,128)(2,1)S(1)} %get-tuple-element.142), channel_id=1, source_target_pairs={{0,2},{1,3},{2,0},{3,1},{4,6},{5,7},{6,4},{7,5},{8,10},{9,11},{10,... | collective-permute-start | bytes 184328 | tf_op jit(solution)/shard_map/ppermute | solution.py:462
  (166 shorter events, 63.8 us)
Async XLA Ops:
  0.7 23.6 %collective-permute-start.2 = (bf16[2,512,640]{2,1,0:T(8,128)(2,1)}, bf16[2,512,640]{2,1,0:T(8,128)(2,1)S(1)}, u32[]{:S(2)}, u32[]{:S(2)}) collective-permute-start(bf16[2,512,640]{2,1,0:T(8,128)(2,1)} %param.20), channel_id=1, source_target_pairs={{0,4},{4,8},{8,12},{12,16},{16,20},{20,24},{24,28},{1,5},{5,9},{9,... | collective-permute-start | bytes 3932168 | tf_op jit(solution)/shard_map/ppermute | solution.py:457
  6.1 9.2 %collective-permute-start = (bf16[1,160,320]{2,1,0:T(8,128)(2,1)S(1)}, bf16[1,160,320]{2,1,0:T(8,128)(2,1)S(1)}, u32[]{:S(2)}, u32[]{:S(2)}) collective-permute-start(bf16[1,160,320]{2,1,0:T(8,128)(2,1)S(1)} %maximum_bitcast_fusion), channel_id=1, source_target_pairs={{0,2},{1,3},{2,0},{3,1},{4,6},{5,7},{6,4},{7,5},{8,10},{9,11},{10,... | collective-permute-start | bytes 307208 | tf_op jit(solution)/shard_map/ppermute | solution.py:462
  9.6 14.7 %collective-permute-start.3 = (s32[2,512]{1,0:T(2,128)}, s32[2,512]{1,0:T(2,128)S(1)}, u32[]{:S(2)}, u32[]{:S(2)}) collective-permute-start(s32[2,512]{1,0:T(2,128)} %param.21), channel_id=1, source_target_pairs={{0,4},{4,8},{8,12},{12,16},{16,20},{20,24},{24,28},{1,5},{5,9},{9,... | collective-permute-start | bytes 12296 | tf_op jit(solution)/shard_map/ppermute | solution.py:457
  15.4 8.8 %collective-permute-start.1 = (bf16[2,160,320]{2,1,0:T(8,128)(2,1)S(1)}, bf16[2,160,320]{2,1,0:T(8,128)(2,1)S(1)}, u32[]{:S(2)}, u32[]{:S(2)}) collective-permute-start(bf16[2,160,320]{2,1,0:T(8,128)(2,1)S(1)} %pad_maximum_fusion.5), channel_id=1, source_target_pairs={{0,1},{1,0},{2,3},{3,2},{4,5},{5,4},{6,7},{7,6},{8,9},{9,8},{10,11... | collective-permute-start | bytes 614408 | tf_op jit(solution)/shard_map/ppermute | solution.py:462
  24.4 15.4 %collective-permute-start.5 = (bf16[4,160,320]{2,1,0:T(8,128)(2,1)S(1)}, bf16[4,160,320]{2,1,0:T(8,128)(2,1)S(1)}, u32[]{:S(2)}, u32[]{:S(2)}) collective-permute-start(bf16[4,160,320]{2,1,0:T(8,128)(2,1)S(1)} %pad_maximum_fusion.2.refs_0_), channel_id=1, source_target_pairs={{0,16},{4,12},{8,24},{12,4},{16,0},{20,28},{24,8},{28,20},{1,17},{... | collective-permute-start | bytes 1228808 | tf_op jit(solution)/shard_map/ppermute | solution.py:462
  26.7 13.0 %collective-permute-start.4 = (bf16[1,480,256]{2,1,0:T(8,128)(2,1)S(1)}, bf16[1,480,256]{2,1,0:T(8,128)(2,1)S(1)}, u32[]{:S(2)}, u32[]{:S(2)}) collective-permute-start(bf16[1,480,256]{2,1,0:T(8,128)(2,1)S(1)} %bitcast.123), channel_id=1, source_target_pairs={{0,2},{1,3},{2,0},{3,1},{4,6},{5,7},{6,4},{7,5},{8,10},{9,11},{10,... | collective-permute-start | bytes 737288 | tf_op jit(solution)/shard_map/ppermute | solution.py:462
  39.7 12.3 %collective-permute-start.8 = (bf16[2,480,256]{2,1,0:T(8,128)(2,1)S(1)}, bf16[2,480,256]{2,1,0:T(8,128)(2,1)S(1)}, u32[]{:S(2)}, u32[]{:S(2)}) collective-permute-start(bf16[2,480,256]{2,1,0:T(8,128)(2,1)S(1)} %pad_maximum_fusion.3), channel_id=1, source_target_pairs={{0,1},{1,0},{2,3},{3,2},{4,5},{5,4},{6,7},{7,6},{8,9},{9,8},{10,11... | collective-permute-start | bytes 1474568 | tf_op jit(solution)/shard_map/ppermute | solution.py:462
  41.1 8.9 %collective-permute-start.6 = (bf16[4,160,320]{2,1,0:T(8,128)(2,1)S(1)}, bf16[4,160,320]{2,1,0:T(8,128)(2,1)}, u32[]{:S(2)}, u32[]{:S(2)}) collective-permute-start(bf16[4,160,320]{2,1,0:T(8,128)(2,1)S(1)} %pad_maximum_fusion.2.refs_0_), channel_id=1, source_target_pairs={{0,8},{4,20},{8,0},{12,28},{16,24},{20,4},{24,16},{28,12},{1,9},{5... | collective-permute-start | bytes 1228808 | tf_op jit(solution)/shard_map/ppermute | solution.py:462
  42.2 14.9 %collective-permute-start.9 = (bf16[4,160,320]{2,1,0:T(8,128)(2,1)S(1)}, bf16[4,160,320]{2,1,0:T(8,128)(2,1)}, u32[]{:S(2)}, u32[]{:S(2)}) collective-permute-start(bf16[4,160,320]{2,1,0:T(8,128)(2,1)S(1)} %pad_maximum_fusion.2.refs_0_), channel_id=1, source_target_pairs={{0,4},{4,0},{8,12},{12,8},{16,20},{20,16},{24,28},{28,24},{1,5},{5... | collective-permute-start | bytes 1228808 | tf_op jit(solution)/shard_map/ppermute | solution.py:462
  42.2 13.2 %collective-permute-start.7 = (bf16[4,160,320]{2,1,0:T(8,128)(2,1)S(1)}, bf16[4,160,320]{2,1,0:T(8,128)(2,1)}, u32[]{:S(2)}, u32[]{:S(2)}) collective-permute-start(bf16[4,160,320]{2,1,0:T(8,128)(2,1)S(1)} %collective-permute-done.5.refs_1_), channel_id=1, source_target_pairs={{0,8},{4,20},{8,0},{12,28},{16,24},{20,4},{24,16},{28,12},{1,9},{5... | collective-permute-start | bytes 1228808 | tf_op jit(solution)/shard_map/ppermute | solution.py:462
  44.8 12.3 %collective-permute-start.10 = (bf16[4,160,320]{2,1,0:T(8,128)(2,1)S(1)}, bf16[4,160,320]{2,1,0:T(8,128)(2,1)}, u32[]{:S(2)}, u32[]{:S(2)}) collective-permute-start(bf16[4,160,320]{2,1,0:T(8,128)(2,1)S(1)} %collective-permute-done.5.refs_1_), channel_id=1, source_target_pairs={{0,4},{4,0},{8,12},{12,8},{16,20},{20,16},{24,28},{28,24},{1,5},{5... | collective-permute-start | bytes 1228808 | tf_op jit(solution)/shard_map/ppermute | solution.py:462
  50.1 7.1 %collective-permute-start.11 = (bf16[4,160,320]{2,1,0:T(8,128)(2,1)}, bf16[4,160,320]{2,1,0:T(8,128)(2,1)}, u32[]{:S(2)}, u32[]{:S(2)}) collective-permute-start(bf16[4,160,320]{2,1,0:T(8,128)(2,1)} %collective-permute-done.6.refs_2_), channel_id=1, source_target_pairs={{0,4},{4,0},{8,12},{12,8},{16,20},{20,16},{24,28},{28,24},{1,5},{5... | collective-permute-start | bytes 1228808 | tf_op jit(solution)/shard_map/ppermute | solution.py:462
  56.5 14.1 %collective-permute-start.13 = (bf16[4,480,256]{2,1,0:T(8,128)(2,1)S(1)}, bf16[4,480,256]{2,1,0:T(8,128)(2,1)S(1)}, u32[]{:S(2)}, u32[]{:S(2)}) collective-permute-start(bf16[4,480,256]{2,1,0:T(8,128)(2,1)S(1)} %pad_maximum_fusion.1.refs_0_), channel_id=1, source_target_pairs={{0,16},{4,12},{8,24},{12,4},{16,0},{20,28},{24,8},{28,20},{1,17},{... | collective-permute-start | bytes 2949128 | tf_op jit(solution)/shard_map/ppermute | solution.py:462
  57.0 39.5 %collective-permute-start.16 = (bf16[4,480,256]{2,1,0:T(8,128)(2,1)S(1)}, bf16[4,480,256]{2,1,0:T(8,128)(2,1)}, u32[]{:S(2)}, u32[]{:S(2)}) collective-permute-start(bf16[4,480,256]{2,1,0:T(8,128)(2,1)S(1)} %pad_maximum_fusion.1.refs_0_), channel_id=1, source_target_pairs={{0,4},{4,0},{8,12},{12,8},{16,20},{20,16},{24,28},{28,24},{1,5},{5... | collective-permute-start | bytes 2949128 | tf_op jit(solution)/shard_map/ppermute | solution.py:462
  70.6 24.7 %collective-permute-start.15 = (bf16[4,480,256]{2,1,0:T(8,128)(2,1)S(1)}, bf16[4,480,256]{2,1,0:T(8,128)(2,1)}, u32[]{:S(2)}, u32[]{:S(2)}) collective-permute-start(bf16[4,480,256]{2,1,0:T(8,128)(2,1)S(1)} %collective-permute-done.13.refs_1_), channel_id=1, source_target_pairs={{0,8},{4,20},{8,0},{12,28},{16,24},{20,4},{24,16},{28,12},{1,9},{5... | collective-permute-start | bytes 2949128 | tf_op jit(solution)/shard_map/ppermute | solution.py:462
  71.0 25.5 %collective-permute-start.17 = (bf16[4,480,256]{2,1,0:T(8,128)(2,1)S(1)}, bf16[4,480,256]{2,1,0:T(8,128)(2,1)}, u32[]{:S(2)}, u32[]{:S(2)}) collective-permute-start(bf16[4,480,256]{2,1,0:T(8,128)(2,1)S(1)} %collective-permute-done.13.refs_1_), channel_id=1, source_target_pairs={{0,4},{4,0},{8,12},{12,8},{16,20},{20,16},{24,28},{28,24},{1,5},{5... | collective-permute-start | bytes 2949128 | tf_op jit(solution)/shard_map/ppermute | solution.py:462
  71.0 24.3 %collective-permute-start.14 = (bf16[4,480,256]{2,1,0:T(8,128)(2,1)S(1)}, bf16[4,480,256]{2,1,0:T(8,128)(2,1)}, u32[]{:S(2)}, u32[]{:S(2)}) collective-permute-start(bf16[4,480,256]{2,1,0:T(8,128)(2,1)S(1)} %pad_maximum_fusion.1.refs_0_), channel_id=1, source_target_pairs={{0,8},{4,20},{8,0},{12,28},{16,24},{20,4},{24,16},{28,12},{1,9},{5... | collective-permute-start | bytes 2949128 | tf_op jit(solution)/shard_map/ppermute | solution.py:462
  163.8 9.9 %collective-permute-start.20 = (bf16[4,4,320,256]{3,2,1,0:T(8,128)(2,1)}, bf16[4,4,320,256]{3,2,1,0:T(8,128)(2,1)}, u32[]{:S(2)}, u32[]{:S(2)}) collective-permute-start(bf16[4,4,320,256]{3,2,1,0:T(8,128)(2,1)} %get-tuple-element.106), channel_id=1, source_target_pairs={{0,4},{4,0},{8,12},{12,8},{16,20},{20,16},{24,28},{28,24},{1,5},{5... | collective-permute-start | bytes 7864328 | tf_op jit(solution)/shard_map/ppermute | solution.py:462
  164.0 7.9 %collective-permute-start.21 = (bf16[4,4,240,256]{3,2,1,0:T(8,128)(2,1)}, bf16[4,4,240,256]{3,2,1,0:T(8,128)(2,1)}, u32[]{:S(2)}, u32[]{:S(2)}) collective-permute-start(bf16[4,4,240,256]{3,2,1,0:T(8,128)(2,1)} %get-tuple-element.108), channel_id=1, source_target_pairs={{0,4},{4,0},{8,12},{12,8},{16,20},{20,16},{24,28},{28,24},{1,5},{5... | collective-permute-start | bytes 5898248 | tf_op jit(solution)/shard_map/ppermute | solution.py:462
  176.8 28.4 %collective-permute-start.22 = (bf16[2,4,560,256]{3,2,1,0:T(8,128)(2,1)}, bf16[2,4,560,256]{3,2,1,0:T(8,128)(2,1)S(1)}, u32[]{:S(2)}, u32[]{:S(2)}) collective-permute-start(bf16[2,4,560,256]{3,2,1,0:T(8,128)(2,1)} %pad_maximum_fusion._), channel_id=1, source_target_pairs={{0,8},{4,20},{8,0},{12,28},{16,24},{20,4},{24,16},{28,12},{1,9},{5... | collective-permute-start | bytes 6881288 | tf_op jit(solution)/shard_map/ppermute | solution.py:462
  193.5 13.5 %collective-permute-start.25 = (bf16[2,512,512]{2,1,0:T(8,128)(2,1)}, bf16[2,512,512]{2,1,0:T(8,128)(2,1)}, u32[]{:S(2)}, u32[]{:S(2)}) collective-permute-start(bf16[2,512,512]{2,1,0:T(8,128)(2,1)} %get-tuple-element.116), channel_id=1, source_target_pairs={{4,0},{8,4},{12,8},{16,12},{20,16},{24,20},{28,24},{5,1},{9,5},{13... | collective-permute-start | bytes 3145736 | tf_op jit(solution)/shard_map/ppermute | solution.py:457
  206.5 28.7 %collective-permute-start.23 = (bf16[4,560,256]{2,1,0:T(8,128)(2,1)}, bf16[4,560,256]{2,1,0:T(8,128)(2,1)}, u32[]{:S(2)}, u32[]{:S(2)}) collective-permute-start(bf16[4,560,256]{2,1,0:T(8,128)(2,1)} %fusion._.refs_1_), channel_id=1, source_target_pairs={{0,16},{4,12},{8,24},{12,4},{16,0},{20,28},{24,8},{28,20},{1,17},{... | collective-permute-start | bytes 3440648 | tf_op jit(solution)/shard_map/ppermute | solution.py:462
  216.3 21.0 %collective-permute-start.26 = (bf16[4,4,160,192]{3,2,1,0:T(8,128)(2,1)}, bf16[4,4,160,192]{3,2,1,0:T(8,128)(2,1)}, u32[]{:S(2)}, u32[]{:S(2)}) collective-permute-start(bf16[4,4,160,192]{3,2,1,0:T(8,128)(2,1)} %attn_gradients_sent.1), channel_id=1, source_target_pairs={{0,4},{4,0},{8,12},{12,8},{16,20},{20,16},{24,28},{28,24},{1,5},{5... | collective-permute-start | bytes 2949128 | tf_op jit(solution)/shard_map/ppermute | solution.py:462
  243.0 10.8 %collective-permute-start.27 = (bf16[2,4,160,192]{3,2,1,0:T(8,128)(2,1)}, bf16[2,4,160,192]{3,2,1,0:T(8,128)(2,1)S(1)}, u32[]{:S(2)}, u32[]{:S(2)}) collective-permute-start(bf16[2,4,160,192]{3,2,1,0:T(8,128)(2,1)} %get-tuple-element.119), channel_id=1, source_target_pairs={{0,8},{4,20},{8,0},{12,28},{16,24},{20,4},{24,16},{28,12},{1,9},{5... | collective-permute-start | bytes 1474568 | tf_op jit(solution)/shard_map/ppermute | solution.py:462
  244.6 13.8 %collective-permute-start.24 = (bf16[2,560,256]{2,1,0:T(8,128)(2,1)}, bf16[2,560,256]{2,1,0:T(8,128)(2,1)S(1)}, u32[]{:S(2)}, u32[]{:S(2)}) collective-permute-start(bf16[2,560,256]{2,1,0:T(8,128)(2,1)} %fusion.2.refs_1_), channel_id=1, source_target_pairs={{0,1},{1,0},{2,3},{3,2},{4,5},{5,4},{6,7},{7,6},{8,9},{9,8},{10,11... | collective-permute-start | bytes 1720328 | tf_op jit(solution)/shard_map/ppermute | solution.py:462
  260.4 13.5 %collective-permute-start.29 = (bf16[4,160,192]{2,1,0:T(8,128)(2,1)}, bf16[4,160,192]{2,1,0:T(8,128)(2,1)}, u32[]{:S(2)}, u32[]{:S(2)}) collective-permute-start(bf16[4,160,192]{2,1,0:T(8,128)(2,1)} %fusion.10.__), channel_id=1, source_target_pairs={{0,16},{4,12},{8,24},{12,4},{16,0},{20,28},{24,8},{28,20},{1,17},{... | collective-permute-start | bytes 737288 | tf_op jit(solution)/shard_map/ppermute | solution.py:462
  261.2 23.2 %collective-permute-start.28 = (bf16[560,256]{1,0:T(8,128)(2,1)}, bf16[560,256]{1,0:T(8,128)(2,1)}, u32[]{:S(2)}, u32[]{:S(2)}) collective-permute-start(bf16[560,256]{1,0:T(8,128)(2,1)} %fusion.6._), channel_id=1, source_target_pairs={{0,2},{1,3},{2,0},{3,1},{4,6},{5,7},{6,4},{7,5},{8,10},{9,11},{10,... | collective-permute-start | bytes 860168 | tf_op jit(solution)/shard_map/ppermute | solution.py:462
  279.9 7.2 %collective-permute-start.31 = (bf16[160,192]{1,0:T(8,128)(2,1)S(1)}, bf16[160,192]{1,0:T(8,128)(2,1)S(1)}, u32[]{:S(2)}, u32[]{:S(2)}) collective-permute-start(bf16[160,192]{1,0:T(8,128)(2,1)S(1)} %get-tuple-element.140), channel_id=1, source_target_pairs={{0,3},{1,2},{2,1},{3,0},{4,7},{5,6},{6,5},{7,4},{8,11},{9,10},{10,... | collective-permute-start | bytes 184328 | tf_op jit(solution)/shard_map/ppermute | solution.py:462
  280.8 7.0 %collective-permute-start.32 = (bf16[160,192]{1,0:T(8,128)(2,1)S(1)}, bf16[160,192]{1,0:T(8,128)(2,1)S(1)}, u32[]{:S(2)}, u32[]{:S(2)}) collective-permute-start(bf16[160,192]{1,0:T(8,128)(2,1)S(1)} %get-tuple-element.141), channel_id=1, source_target_pairs={{0,1},{1,0},{2,3},{3,2},{4,5},{5,4},{6,7},{7,6},{8,9},{9,8},{10,11... | collective-permute-start | bytes 184328 | tf_op jit(solution)/shard_map/ppermute | solution.py:462
  281.2 7.3 %collective-permute-start.33 = (bf16[160,192]{1,0:T(8,128)(2,1)S(1)}, bf16[160,192]{1,0:T(8,128)(2,1)S(1)}, u32[]{:S(2)}, u32[]{:S(2)}) collective-permute-start(bf16[160,192]{1,0:T(8,128)(2,1)S(1)} %get-tuple-element.142), channel_id=1, source_target_pairs={{0,2},{1,3},{2,0},{3,1},{4,6},{5,7},{6,4},{7,5},{8,10},{9,11},{10,... | collective-permute-start | bytes 184328 | tf_op jit(solution)/shard_map/ppermute | solution.py:462
  288.5 8.6 %collective-permute-start.37 = (f32[8,640]{1,0:T(8,128)S(1)}, f32[8,640]{1,0:T(8,128)S(1)}, u32[]{:S(2)}, u32[]{:S(2)}) collective-permute-start(f32[8,640]{1,0:T(8,128)S(1)} %add_add_fusion.1), channel_id=1, source_target_pairs={{0,1},{1,0},{2,3},{3,2},{4,5},{5,4},{6,7},{7,6},{8,9},{9,8},{10,11... | collective-permute-start | bytes 61448 | tf_op jit(solution)/shard_map/ppermute | solution.py:462
  290.0 7.1 %collective-permute-start.38 = (f32[8,640]{1,0:T(8,128)S(1)}, f32[8,640]{1,0:T(8,128)S(1)}, u32[]{:S(2)}, u32[]{:S(2)}) collective-permute-start(f32[8,640]{1,0:T(8,128)S(1)} %add_add_fusion.1), channel_id=1, source_target_pairs={{0,2},{1,3},{2,0},{3,1},{4,6},{5,7},{6,4},{7,5},{8,10},{9,11},{10,... | collective-permute-start | bytes 61448 | tf_op jit(solution)/shard_map/ppermute | solution.py:462
  (27 other events, 401.9 us)

commit v2 on v1

--- a/solution.py
+++ b/solution.py
@@ -433,7 +433,7 @@
 
 
 def input_kernel(
-    _, __, gq_ref, gkv_ref, wq_ref, wkv_ref, tok_ref, gres_ref, gains_ref, ffn_gain_ref, kgain_ref,
+    _, gq_ref, gkv_ref, wq_ref, wkv_ref, tok_ref, gres_ref, gains_ref, ffn_gain_ref, kgain_ref,
     qgain_ref, dtok_ref, gain_ref
 ):
     @pl.when(pl.program_id(0) == 0)
@@ -885,7 +885,8 @@
     g_recv = passed_along(g_far, "seq", -1)
     early = ffn
     if exchange.direct:
-        ffn = early = exchange.fold(*ffn, 1)
+        ffn, g_recv = linked(exchange.fold(*ffn, 1), g_recv)
+        early = ffn
     g_kv, key_gain = pl.pallas_call(
         kv_back_kernel,
         grid=(seq_dev,),
@@ -928,12 +929,10 @@
         ffn = exchange.fold(*ffn, 2)
     attn_parts_kept = attn_parts(half, ffn[0], [attn_got])
     attn = attn_parts_kept[0], [(attn_parts_kept[1], 1)]
-    if exchange.direct:
-        ffn, attn = linked(exchange.fold(*ffn, 3), exchange.fold(*attn, 1))
     dtokens, sums = pl.pallas_call(
         input_kernel,
         grid=(seq_dev,),
-        in_specs=[remain, remain, rows(block, inner), rows(block, 2 * head_dim)]
+        in_specs=[remain, rows(block, inner), rows(block, 2 * head_dim)]
         + [wq_spec, wkv_spec]
         + [tok_spec, tok_spec, gains_spec, whole((8, width))]
         + [whole((8, head_dim))] * 2,
@@ -942,16 +941,16 @@
         compiler_params=params(),
         name="input_gradient",
         cost_estimate=cost(7),
-    )(ffn[0], attn[0], g_query, g_kv, full_q, full_kv, tokens_2d, g_res, gains, ffn_gains, key_gain, query_gain)
+    )(attn_parts_kept[0], g_query, g_kv, full_q, full_kv, tokens_2d, g_res, gains, ffn_gains, key_gain, query_gain)
 
     if exchange.direct:
-        attn = exchange.hop_terms(*attn)
+        ffn, attn = exchange.fold(*ffn, 3), exchange.fold(*attn, 1)
         sums = exchange.hop(sums, "seq", (1,))
+        ffn, attn, sums = linked(ffn, attn, sums)
+        ffn, attn = exchange.fold(*ffn, 4), exchange.hop_terms(*attn)
+        sums = exchange.hop(sums, "seq", (2, 4))
         *attn, sums = linked(*attn, sums)
         attn = exchange.last(*attn)
-        sums = exchange.hop(sums, "seq", (2, 4))
-        ffn = exchange.fold(*ffn, 4)
-        ffn, attn, sums = linked(ffn, attn, sums)
         sums = exchange.hop(sums, "fsdp", (1, 2))
         weights = split_gradients(ffn, attn)
     else:

time: 299 us -> 285 us (0.953)
  starting transfers between devices: 61.8 us -> 53.9 us
  waiting for transfers between devices: 69.4 us -> 65.5 us
    ppermute x37, starting transfers between devices: 54.6 us -> 46.7 us  [swapped(): lax.ppermute(array, axis, [(i, i ^ (odd if i % 2 else even)) for i in ran...]
    ppermute x37, waiting for transfers between devices: 69.4 us -> 65.5 us  [swapped(): lax.ppermute(array, axis, [(i, i ^ (odd if i % 2 else even)) for i in ran...]
  transfers between devices with their start and end apart: 40 -> 40, of which waited for: 20 -> 19; matrix products, arithmetic and copies ran while one was open for 11% -> 11% of each run, Pallas kernels for 19% -> 22%
where the time goes in v2:
time: 285 us; the launch traced here: 284 us
  Pallas kernels  125 us (44%)
  waiting for transfers between devices  65.5 us (23%)
  starting transfers between devices  53.9 us (19%)
  other arithmetic  26.6 us (9%)
  local copies, waits for them, and re-layouts  11.5 us (4%)
    ppermute x37, waiting for transfers between devices, swapped(): lax.ppermute(array, axis, [(i, i ^ (odd if i % 2 else even)) for i in ran...  65.5 us
    pallas_call x1, Pallas kernels, body(): pl.pallas_call(ffn_kernel, grid=(tiles + pieces,), in_specs=[smem, smem,...  64.1 us
    ppermute x37, starting transfers between devices, swapped(): lax.ppermute(array, axis, [(i, i ^ (odd if i % 2 else even)) for i in ran...  46.7 us
    pallas_call x1, Pallas kernels, body(): pl.pallas_call(attn_back_kernel, grid=(seq_dev,), in_specs=[remain, rows(...  16.3 us
    pallas_call x1, Pallas kernels, body(): pl.pallas_call(attn_kernel, grid=(seq_dev,), in_specs=[rows(block, inner)...  12.1 us
    pallas_call x2, Pallas kernels, attn_parts(): pl.pallas_call(lambda *refs: attn_grad_kernel(base, *refs), in_specs=[sme...  11.1 us
    add x11, other arithmetic, total(): result = result + term.astype(f32)  11.1 us
    pallas_call x1, Pallas kernels, body(): pl.pallas_call(qkv_kernel, grid=(seq_dev,), in_specs=[smem, tok_spec, tok...  11 us
  transfers between devices with their start and end apart: 40, of which 19 were waited for; matrix products, arithmetic and copies ran while one was open for 11% of the time, Pallas kernels for 22%

profile of v2, /device:TPU:0, one launch (start us, length us, event | category | flops | bytes accessed | tf_op | source)
XLA Modules:
  0.0 283.9 jit_solution(1109445857531487876)
XLA Ops:
  0.7 2.6 collective-permute-start.2
  6.1 3.5 %collective-permute-start = (bf16[1,160,320]{2,1,0:T(8,128)(2,1)S(1)}, bf16[1,160,320]{2,1,0:T(8,128)(2,1)S(1)}, u32[]{:S(2)}, u32[]{:S(2)}) collective-permute-start(bf16[1,160,320]{2,1,0:T(8,128)(2,1)S(1)} %maximum_bitcast_fusion), channel_id=1, source_target_pairs={{0,2},{1,3},{2,0},{3,1},{4,6},{5,7},{6,4},{7,5},{8,10},{9,11},{10,... | collective-permute-start | bytes 307208 | tf_op jit(solution)/shard_map/ppermute | solution.py:462
  9.6 3.3 %collective-permute-start.3 = (s32[2,512]{1,0:T(2,128)}, s32[2,512]{1,0:T(2,128)S(1)}, u32[]{:S(2)}, u32[]{:S(2)}) collective-permute-start(s32[2,512]{1,0:T(2,128)} %param.21), channel_id=1, source_target_pairs={{0,4},{4,8},{8,12},{12,16},{16,20},{20,24},{24,28},{1,5},{5,9},{9,... | collective-permute-start | bytes 12296 | tf_op jit(solution)/shard_map/ppermute | solution.py:457
  13.2 2.2 collective-permute-done
  15.4 2.1 collective-permute-start.1
  18.4 5.8 %collective-permute-done.1 = bf16[2,160,320]{2,1,0:T(8,128)(2,1)S(1)} collective-permute-done((bf16[2,160,320]{2,1,0:T(8,128)(2,1)S(1)}, bf16[2,160,320]{2,1,0:T(8,128)(2,1)S(1)}, u32[]{:S(2)}, u32[]{:S(2)}) %collective-permute-start.1) | collective-permute-done | bytes 204832 | tf_op jit(solution)/shard_map/ppermute | solution.py:462
  24.4 2.3 collective-permute-start.5
  26.7 2.3 collective-permute-start.4
  29.7 10.0 %collective-permute-done.4 = bf16[1,480,256]{2,1,0:T(8,128)(2,1)S(1)} collective-permute-done((bf16[1,480,256]{2,1,0:T(8,128)(2,1)S(1)}, bf16[1,480,256]{2,1,0:T(8,128)(2,1)S(1)}, u32[]{:S(2)}, u32[]{:S(2)}) %collective-permute-start.4) | collective-permute-done | bytes 245792 | tf_op jit(solution)/shard_map/ppermute | solution.py:462
  45.2 4.9 %collective-permute-done.6.refs_2_ = bf16[4,160,320]{2,1,0:T(8,128)(2,1)} collective-permute-done((bf16[4,160,320]{2,1,0:T(8,128)(2,1)S(1)}, bf16[4,160,320]{2,1,0:T(8,128)(2,1)}, u32[]{:S(2)}, u32[]{:S(2)}) %collective-permute-start.6) | collective-permute-done | bytes 409632 | tf_op jit(solution)/shard_map/ppermute | solution.py:462
  50.1 2.0 collective-permute-done.8
  52.2 3.2 %collective-permute-done.7.refs_3_ = bf16[4,160,320]{2,1,0:T(8,128)(2,1)} collective-permute-done((bf16[4,160,320]{2,1,0:T(8,128)(2,1)S(1)}, bf16[4,160,320]{2,1,0:T(8,128)(2,1)}, u32[]{:S(2)}, u32[]{:S(2)}) %collective-permute-start.7) | collective-permute-done | bytes 409632 | tf_op jit(solution)/shard_map/ppermute | solution.py:462
  57.6 11.0 %project_rotate.1 = (bf16[1024,640]{1,0:T(8,128)(2,1)}, f32[1024,1024]{1,0:T(8,128)}, bf16[1024,1024]{1,0:T(8,128)(2,1)}, f32[1024,256]{1,0:T(8,128)}, bf16[2,10...) custom-call(s32[12]{0:T(128)} %stack.92.held_ref, ...), custom_call_target="tpu_custom_call" | custom-call | flops 11000000512 | bytes 33000000 | tf_op jit(solution)/shard_map/project_rotate/pallas_call | solution.py:729
  68.6 2.0 collective-permute-done.13.refs_1_
  72.6 12.1 %window_attention.1 = (bf16[1024,1024]{1,0:T(8,128)(2,1)}, f32[1024,128]{1,0:T(8,128)}, f32[1024,640]{1,0:T(8,128)}, f32[1024,640]{1,0:T(8,128)}, bf16[1024,640]{1,0:T(8,128)(2,1)}) custom-call(bf16[1024,1024]{1,0:T(8,128)(2,1)} %get-tuple-element.93.q_ref, bf16[2,1024,256]{2,1,0:T(8,128)(2,1)} %get-tuple-element.96.key_ref, ...), custom_call_target="tpu_custom_call" | custom-call | flops 12000000000 | bytes 36000000 | tf_op jit(solution)/shard_map/window_attention/pallas_call | solution.py:770
  84.7 10.6 %collective-permute-done.14.refs_2_ = bf16[4,480,256]{2,1,0:T(8,128)(2,1)} collective-permute-done((bf16[4,480,256]{2,1,0:T(8,128)(2,1)S(1)}, bf16[4,480,256]{2,1,0:T(8,128)(2,1)}, u32[]{:S(2)}, u32[]{:S(2)}) %collective-permute-start.14) | collective-permute-done | bytes 983072 | tf_op jit(solution)/shard_map/ppermute | solution.py:462
  99.6 64.1 %feed_forward.1 = (bf16[1024,640]{1,0:T(8,128)(2,1)}, f32[1024,640]{1,0:T(8,128)}, bf16[1024,1024]{1,0:T(8,128)(2,1)}, f32[8,640]{1,0:T(8,128)}, bf16[4,4,320,25...) custom-call(s32[12]{0:T(128)} %stack.92.held_ref, ...), custom_call_target="tpu_custom_call" | custom-call | flops 60000002048 | bytes 180000000 | tf_op jit(solution)/shard_map/feed_forward/pallas_call | solution.py:820
  164.8 7.2 %collective-permute-done.21 = bf16[4,4,240,256]{3,2,1,0:T(8,128)(2,1)} collective-permute-done((bf16[4,4,240,256]{3,2,1,0:T(8,128)(2,1)}, bf16[4,4,240,256]{3,2,1,0:T(8,128)(2,1)}, u32[]{:S(2)}, u32[]{:S(2)}) %collective-permute-start.21) | collective-permute-done | bytes 1966112 | tf_op jit(solution)/shard_map/ppermute | solution.py:462
  177.2 16.3 %attention_gradient.1 = (bf16[1024,1024]{1,0:T(8,128)(2,1)}, bf16[2,512,512]{2,1,0:T(8,128)(2,1)}, f32[2,512,512]{2,1,0:T(8,128)}, f32[8,256]{1,0:T(8,128)}) custom-call(bf16[2,4,560,256]{3,2,1,0:T(8,128)(2,1)} %pad_maximum_fusion._, bf16[1024,1024]{1,0:T(8,128)(2,1)} %get-tuple-element.93.q_ref, bf16[1024,1024]{1,0:T(8,128)(2,1)} %get-tuple-element.114.gctx_ref, ...), custom_call_target="tpu_custom_call" | custom-call | flops 16000000000 | bytes 48000000 | tf_op jit(solution)/shard_map/attention_gradient/pallas_call | solution.py:861
  198.2 7.0 %collective-permute-done.22 = bf16[2,4,560,256]{3,2,1,0:T(8,128)(2,1)S(1)} collective-permute-done((bf16[2,4,560,256]{3,2,1,0:T(8,128)(2,1)}, bf16[2,4,560,256]{3,2,1,0:T(8,128)(2,1)S(1)}, u32[]{:S(2)}, u32[]{:S(2)}) %collective-permute-start.22) | collective-permute-done | bytes 2293792 | tf_op jit(solution)/shard_map/ppermute | solution.py:462
  206.5 9.7 %collective-permute-start.24 = (bf16[4,560,256]{2,1,0:T(8,128)(2,1)}, bf16[4,560,256]{2,1,0:T(8,128)(2,1)}, u32[]{:S(2)}, u32[]{:S(2)}) collective-permute-start(bf16[4,560,256]{2,1,0:T(8,128)(2,1)} %fusion._.refs_1_), channel_id=1, source_target_pairs={{0,16},{4,12},{8,24},{12,4},{16,0},{20,28},{24,8},{28,20},{1,17},{... | collective-permute-start | bytes 3440648 | tf_op jit(solution)/shard_map/ppermute | solution.py:462
  216.2 3.6 %key_value_back.1 = (bf16[1024,512]{1,0:T(8,128)(2,1)}, f32[8,256]{1,0:T(8,128)}) custom-call(f32[1024,256]{1,0:T(8,128)} %get-tuple-element.126.kraw_ref, f32[512,128]{1,0:T(8,128)} %constant.82.clone.cos_ref, f32[512,128]{1,0:T(8,128)} %constant.83.clone.sin_ref, f32[2,256]{1,0:T(2,128)} %pad_maximum_fusion.8.head_ref, ...), custom_call_target="tpu_custom_call" | custom-call | flops 4000000000 | bytes 12000000 | tf_op jit(solution)/shard_map/key_value_back/pallas_call | solution.py:890
  219.8 5.4 %attn_gradients_sent.1 = bf16[4,4,160,192]{3,2,1,0:T(8,128)(2,1)} custom-call(s32[12]{0:T(128)} %stack.93.order_ref.refs_0_, bf16[4,560,256]{2,1,0:T(8,128)(2,1)} %fusion._.refs_1_, bf16[1024,640]{1,0:T(8,128)(2,1)} %get-tuple-element.124.refs_2_, bf16[1024,1024]{1,0:T(8,128)(2,1)} %get-tuple-element.125.refs_3_.gq_ref, ...), custom_call_target="tpu_custom_call" | custom-call | flops 6000000000 | bytes 18000000 | tf_op jit(solution)/shard_map/attn_gradients_sent/pallas_call | solution.py:915
  230.4 2.1 fusion.2.refs_1_
  232.5 1.8 collective-permute-start.26
  234.3 5.7 %attn_gradients_kept.1 = (bf16[2,4,160,192]{3,2,1,0:T(8,128)(2,1)}, bf16[2,4,160,192]{3,2,1,0:T(8,128)(2,1)}) custom-call(s32[12]{0:T(128)} %stack.93.order_ref.refs_0_, bf16[2,560,256]{2,1,0:T(8,128)(2,1)} %fusion.2.refs_1_, bf16[1024,640]{1,0:T(8,128)(2,1)} %get-tuple-element.124.refs_2_, bf16[1024,1024]{1,0:T(8,128)(2,1)} %get-tuple-element.125.refs_3_.gq_ref, ...), custom_call_target="tpu_custom_call" | custom-call | flops 6000000000 | bytes 18000000 | tf_op jit(solution)/shard_map/attn_gradients_kept/pallas_call | solution.py:915
  241.4 7.0 %input_gradient.1 = (bf16[1024,640]{1,0:T(8,128)(2,1)}, f32[8,640]{1,0:T(8,128)}) custom-call(bf16[2,4,160,192]{3,2,1,0:T(8,128)(2,1)} %get-tuple-element.130._, bf16[1024,1024]{1,0:T(8,128)(2,1)} %get-tuple-element.125.refs_3_.gq_ref, bf16[1024,512]{1,0:T(8,128)(2,1)} %get-tuple-element.129.refs_4_.gkv_ref, bf16[640,1024]{1,0:T(8,128)(2,1)} %get-tuple-element.131.wq_ref, ...), custom_call_target="tpu_custom_call" | custom-call | flops 7000000000 | bytes 21000000 | tf_op jit(solution)/shard_map/input_gradient/pallas_call | solution.py:932
  256.8 2.0 collective-permute-start.29
  261.4 2.6 collective-permute-done.29
  265.4 3.4 %collective-permute-start.38 = (f32[8,640]{1,0:T(8,128)S(1)}, f32[8,640]{1,0:T(8,128)S(1)}, u32[]{:S(2)}, u32[]{:S(2)}) collective-permute-start(f32[8,640]{1,0:T(8,128)S(1)} %add_add_fusion.1), channel_id=1, source_target_pairs={{0,2},{1,3},{2,0},{3,1},{4,6},{5,7},{6,4},{7,5},{8,10},{9,11},{10,... | collective-permute-start | bytes 61448 | tf_op jit(solution)/shard_map/ppermute | solution.py:462
  270.5 3.2 %collective-permute-start.33 = (bf16[160,192]{1,0:T(8,128)(2,1)S(1)}, bf16[160,192]{1,0:T(8,128)(2,1)S(1)}, u32[]{:S(2)}, u32[]{:S(2)}) collective-permute-start(bf16[160,192]{1,0:T(8,128)(2,1)S(1)} %get-tuple-element.145), channel_id=1, source_target_pairs={{0,3},{1,2},{2,1},{3,0},{4,7},{5,6},{6,5},{7,4},{8,11},{9,10},{10,... | collective-permute-start | bytes 184328 | tf_op jit(solution)/shard_map/ppermute | solution.py:462
  273.7 2.0 collective-permute-done.38
  (160 shorter events, 60.0 us)
Async XLA Ops:
  0.7 23.6 %collective-permute-start.2 = (bf16[2,512,640]{2,1,0:T(8,128)(2,1)}, bf16[2,512,640]{2,1,0:T(8,128)(2,1)S(1)}, u32[]{:S(2)}, u32[]{:S(2)}) collective-permute-start(bf16[2,512,640]{2,1,0:T(8,128)(2,1)} %param.20), channel_id=1, source_target_pairs={{0,4},{4,8},{8,12},{12,16},{16,20},{20,24},{24,28},{1,5},{5,9},{9,... | collective-permute-start | bytes 3932168 | tf_op jit(solution)/shard_map/ppermute | solution.py:457
  6.1 9.2 %collective-permute-start = (bf16[1,160,320]{2,1,0:T(8,128)(2,1)S(1)}, bf16[1,160,320]{2,1,0:T(8,128)(2,1)S(1)}, u32[]{:S(2)}, u32[]{:S(2)}) collective-permute-start(bf16[1,160,320]{2,1,0:T(8,128)(2,1)S(1)} %maximum_bitcast_fusion), channel_id=1, source_target_pairs={{0,2},{1,3},{2,0},{3,1},{4,6},{5,7},{6,4},{7,5},{8,10},{9,11},{10,... | collective-permute-start | bytes 307208 | tf_op jit(solution)/shard_map/ppermute | solution.py:462
  9.6 14.7 %collective-permute-start.3 = (s32[2,512]{1,0:T(2,128)}, s32[2,512]{1,0:T(2,128)S(1)}, u32[]{:S(2)}, u32[]{:S(2)}) collective-permute-start(s32[2,512]{1,0:T(2,128)} %param.21), channel_id=1, source_target_pairs={{0,4},{4,8},{8,12},{12,16},{16,20},{20,24},{24,28},{1,5},{5,9},{9,... | collective-permute-start | bytes 12296 | tf_op jit(solution)/shard_map/ppermute | solution.py:457
  15.4 8.8 %collective-permute-start.1 = (bf16[2,160,320]{2,1,0:T(8,128)(2,1)S(1)}, bf16[2,160,320]{2,1,0:T(8,128)(2,1)S(1)}, u32[]{:S(2)}, u32[]{:S(2)}) collective-permute-start(bf16[2,160,320]{2,1,0:T(8,128)(2,1)S(1)} %pad_maximum_fusion.5), channel_id=1, source_target_pairs={{0,1},{1,0},{2,3},{3,2},{4,5},{5,4},{6,7},{7,6},{8,9},{9,8},{10,11... | collective-permute-start | bytes 614408 | tf_op jit(solution)/shard_map/ppermute | solution.py:462
  24.4 15.4 %collective-permute-start.5 = (bf16[4,160,320]{2,1,0:T(8,128)(2,1)S(1)}, bf16[4,160,320]{2,1,0:T(8,128)(2,1)S(1)}, u32[]{:S(2)}, u32[]{:S(2)}) collective-permute-start(bf16[4,160,320]{2,1,0:T(8,128)(2,1)S(1)} %pad_maximum_fusion.2.refs_0_), channel_id=1, source_target_pairs={{0,16},{4,12},{8,24},{12,4},{16,0},{20,28},{24,8},{28,20},{1,17},{... | collective-permute-start | bytes 1228808 | tf_op jit(solution)/shard_map/ppermute | solution.py:462
  26.7 13.0 %collective-permute-start.4 = (bf16[1,480,256]{2,1,0:T(8,128)(2,1)S(1)}, bf16[1,480,256]{2,1,0:T(8,128)(2,1)S(1)}, u32[]{:S(2)}, u32[]{:S(2)}) collective-permute-start(bf16[1,480,256]{2,1,0:T(8,128)(2,1)S(1)} %bitcast.119), channel_id=1, source_target_pairs={{0,2},{1,3},{2,0},{3,1},{4,6},{5,7},{6,4},{7,5},{8,10},{9,11},{10,... | collective-permute-start | bytes 737288 | tf_op jit(solution)/shard_map/ppermute | solution.py:462
  39.7 12.3 %collective-permute-start.8 = (bf16[2,480,256]{2,1,0:T(8,128)(2,1)S(1)}, bf16[2,480,256]{2,1,0:T(8,128)(2,1)S(1)}, u32[]{:S(2)}, u32[]{:S(2)}) collective-permute-start(bf16[2,480,256]{2,1,0:T(8,128)(2,1)S(1)} %pad_maximum_fusion.3), channel_id=1, source_target_pairs={{0,1},{1,0},{2,3},{3,2},{4,5},{5,4},{6,7},{7,6},{8,9},{9,8},{10,11... | collective-permute-start | bytes 1474568 | tf_op jit(solution)/shard_map/ppermute | solution.py:462
  41.1 8.9 %collective-permute-start.6 = (bf16[4,160,320]{2,1,0:T(8,128)(2,1)S(1)}, bf16[4,160,320]{2,1,0:T(8,128)(2,1)}, u32[]{:S(2)}, u32[]{:S(2)}) collective-permute-start(bf16[4,160,320]{2,1,0:T(8,128)(2,1)S(1)} %pad_maximum_fusion.2.refs_0_), channel_id=1, source_target_pairs={{0,8},{4,20},{8,0},{12,28},{16,24},{20,4},{24,16},{28,12},{1,9},{5... | collective-permute-start | bytes 1228808 | tf_op jit(solution)/shard_map/ppermute | solution.py:462
  42.2 14.8 %collective-permute-start.9 = (bf16[4,160,320]{2,1,0:T(8,128)(2,1)S(1)}, bf16[4,160,320]{2,1,0:T(8,128)(2,1)}, u32[]{:S(2)}, u32[]{:S(2)}) collective-permute-start(bf16[4,160,320]{2,1,0:T(8,128)(2,1)S(1)} %pad_maximum_fusion.2.refs_0_), channel_id=1, source_target_pairs={{0,4},{4,0},{8,12},{12,8},{16,20},{20,16},{24,28},{28,24},{1,5},{5... | collective-permute-start | bytes 1228808 | tf_op jit(solution)/shard_map/ppermute | solution.py:462
  42.2 13.2 %collective-permute-start.7 = (bf16[4,160,320]{2,1,0:T(8,128)(2,1)S(1)}, bf16[4,160,320]{2,1,0:T(8,128)(2,1)}, u32[]{:S(2)}, u32[]{:S(2)}) collective-permute-start(bf16[4,160,320]{2,1,0:T(8,128)(2,1)S(1)} %collective-permute-done.5.refs_1_), channel_id=1, source_target_pairs={{0,8},{4,20},{8,0},{12,28},{16,24},{20,4},{24,16},{28,12},{1,9},{5... | collective-permute-start | bytes 1228808 | tf_op jit(solution)/shard_map/ppermute | solution.py:462
  44.8 12.3 %collective-permute-start.10 = (bf16[4,160,320]{2,1,0:T(8,128)(2,1)S(1)}, bf16[4,160,320]{2,1,0:T(8,128)(2,1)}, u32[]{:S(2)}, u32[]{:S(2)}) collective-permute-start(bf16[4,160,320]{2,1,0:T(8,128)(2,1)S(1)} %collective-permute-done.5.refs_1_), channel_id=1, source_target_pairs={{0,4},{4,0},{8,12},{12,8},{16,20},{20,16},{24,28},{28,24},{1,5},{5... | collective-permute-start | bytes 1228808 | tf_op jit(solution)/shard_map/ppermute | solution.py:462
  50.1 7.1 %collective-permute-start.11 = (bf16[4,160,320]{2,1,0:T(8,128)(2,1)}, bf16[4,160,320]{2,1,0:T(8,128)(2,1)}, u32[]{:S(2)}, u32[]{:S(2)}) collective-permute-start(bf16[4,160,320]{2,1,0:T(8,128)(2,1)} %collective-permute-done.6.refs_2_), channel_id=1, source_target_pairs={{0,4},{4,0},{8,12},{12,8},{16,20},{20,16},{24,28},{28,24},{1,5},{5... | collective-permute-start | bytes 1228808 | tf_op jit(solution)/shard_map/ppermute | solution.py:462
  56.5 14.1 %collective-permute-start.13 = (bf16[4,480,256]{2,1,0:T(8,128)(2,1)S(1)}, bf16[4,480,256]{2,1,0:T(8,128)(2,1)S(1)}, u32[]{:S(2)}, u32[]{:S(2)}) collective-permute-start(bf16[4,480,256]{2,1,0:T(8,128)(2,1)S(1)} %pad_maximum_fusion.1.refs_0_), channel_id=1, source_target_pairs={{0,16},{4,12},{8,24},{12,4},{16,0},{20,28},{24,8},{28,20},{1,17},{... | collective-permute-start | bytes 2949128 | tf_op jit(solution)/shard_map/ppermute | solution.py:462
  57.0 39.5 %collective-permute-start.16 = (bf16[4,480,256]{2,1,0:T(8,128)(2,1)S(1)}, bf16[4,480,256]{2,1,0:T(8,128)(2,1)}, u32[]{:S(2)}, u32[]{:S(2)}) collective-permute-start(bf16[4,480,256]{2,1,0:T(8,128)(2,1)S(1)} %pad_maximum_fusion.1.refs_0_), channel_id=1, source_target_pairs={{0,4},{4,0},{8,12},{12,8},{16,20},{20,16},{24,28},{28,24},{1,5},{5... | collective-permute-start | bytes 2949128 | tf_op jit(solution)/shard_map/ppermute | solution.py:462
  70.6 24.7 %collective-permute-start.15 = (bf16[4,480,256]{2,1,0:T(8,128)(2,1)S(1)}, bf16[4,480,256]{2,1,0:T(8,128)(2,1)}, u32[]{:S(2)}, u32[]{:S(2)}) collective-permute-start(bf16[4,480,256]{2,1,0:T(8,128)(2,1)S(1)} %collective-permute-done.13.refs_1_), channel_id=1, source_target_pairs={{0,8},{4,20},{8,0},{12,28},{16,24},{20,4},{24,16},{28,12},{1,9},{5... | collective-permute-start | bytes 2949128 | tf_op jit(solution)/shard_map/ppermute | solution.py:462
  71.0 25.5 %collective-permute-start.17 = (bf16[4,480,256]{2,1,0:T(8,128)(2,1)S(1)}, bf16[4,480,256]{2,1,0:T(8,128)(2,1)}, u32[]{:S(2)}, u32[]{:S(2)}) collective-permute-start(bf16[4,480,256]{2,1,0:T(8,128)(2,1)S(1)} %collective-permute-done.13.refs_1_), channel_id=1, source_target_pairs={{0,4},{4,0},{8,12},{12,8},{16,20},{20,16},{24,28},{28,24},{1,5},{5... | collective-permute-start | bytes 2949128 | tf_op jit(solution)/shard_map/ppermute | solution.py:462
  71.0 24.3 %collective-permute-start.14 = (bf16[4,480,256]{2,1,0:T(8,128)(2,1)S(1)}, bf16[4,480,256]{2,1,0:T(8,128)(2,1)}, u32[]{:S(2)}, u32[]{:S(2)}) collective-permute-start(bf16[4,480,256]{2,1,0:T(8,128)(2,1)S(1)} %pad_maximum_fusion.1.refs_0_), channel_id=1, source_target_pairs={{0,8},{4,20},{8,0},{12,28},{16,24},{20,4},{24,16},{28,12},{1,9},{5... | collective-permute-start | bytes 2949128 | tf_op jit(solution)/shard_map/ppermute | solution.py:462
  163.8 9.9 %collective-permute-start.20 = (bf16[4,4,320,256]{3,2,1,0:T(8,128)(2,1)}, bf16[4,4,320,256]{3,2,1,0:T(8,128)(2,1)}, u32[]{:S(2)}, u32[]{:S(2)}) collective-permute-start(bf16[4,4,320,256]{3,2,1,0:T(8,128)(2,1)} %get-tuple-element.111), channel_id=1, source_target_pairs={{0,4},{4,0},{8,12},{12,8},{16,20},{20,16},{24,28},{28,24},{1,5},{5... | collective-permute-start | bytes 7864328 | tf_op jit(solution)/shard_map/ppermute | solution.py:462
  164.0 7.9 %collective-permute-start.21 = (bf16[4,4,240,256]{3,2,1,0:T(8,128)(2,1)}, bf16[4,4,240,256]{3,2,1,0:T(8,128)(2,1)}, u32[]{:S(2)}, u32[]{:S(2)}) collective-permute-start(bf16[4,4,240,256]{3,2,1,0:T(8,128)(2,1)} %get-tuple-element.113), channel_id=1, source_target_pairs={{0,4},{4,0},{8,12},{12,8},{16,20},{20,16},{24,28},{28,24},{1,5},{5... | collective-permute-start | bytes 5898248 | tf_op jit(solution)/shard_map/ppermute | solution.py:462
  176.8 28.4 %collective-permute-start.22 = (bf16[2,4,560,256]{3,2,1,0:T(8,128)(2,1)}, bf16[2,4,560,256]{3,2,1,0:T(8,128)(2,1)S(1)}, u32[]{:S(2)}, u32[]{:S(2)}) collective-permute-start(bf16[2,4,560,256]{3,2,1,0:T(8,128)(2,1)} %pad_maximum_fusion._), channel_id=1, source_target_pairs={{0,8},{4,20},{8,0},{12,28},{16,24},{20,4},{24,16},{28,12},{1,9},{5... | collective-permute-start | bytes 6881288 | tf_op jit(solution)/shard_map/ppermute | solution.py:462
  193.5 13.0 %collective-permute-start.23 = (bf16[2,512,512]{2,1,0:T(8,128)(2,1)}, bf16[2,512,512]{2,1,0:T(8,128)(2,1)}, u32[]{:S(2)}, u32[]{:S(2)}) collective-permute-start(bf16[2,512,512]{2,1,0:T(8,128)(2,1)} %get-tuple-element.117), channel_id=1, source_target_pairs={{4,0},{8,4},{12,8},{16,12},{20,16},{24,20},{28,24},{5,1},{9,5},{13... | collective-permute-start | bytes 3145736 | tf_op jit(solution)/shard_map/ppermute | solution.py:457
  206.5 23.8 %collective-permute-start.24 = (bf16[4,560,256]{2,1,0:T(8,128)(2,1)}, bf16[4,560,256]{2,1,0:T(8,128)(2,1)}, u32[]{:S(2)}, u32[]{:S(2)}) collective-permute-start(bf16[4,560,256]{2,1,0:T(8,128)(2,1)} %fusion._.refs_1_), channel_id=1, source_target_pairs={{0,16},{4,12},{8,24},{12,4},{16,0},{20,28},{24,8},{28,20},{1,17},{... | collective-permute-start | bytes 3440648 | tf_op jit(solution)/shard_map/ppermute | solution.py:462
  225.2 9.1 %collective-permute-start.25 = (bf16[4,4,160,192]{3,2,1,0:T(8,128)(2,1)}, bf16[4,4,160,192]{3,2,1,0:T(8,128)(2,1)}, u32[]{:S(2)}, u32[]{:S(2)}) collective-permute-start(bf16[4,4,160,192]{3,2,1,0:T(8,128)(2,1)} %attn_gradients_sent.1), channel_id=1, source_target_pairs={{0,4},{4,0},{8,12},{12,8},{16,20},{20,16},{24,28},{28,24},{1,5},{5... | collective-permute-start | bytes 2949128 | tf_op jit(solution)/shard_map/ppermute | solution.py:462
  232.5 19.5 %collective-permute-start.26 = (bf16[2,560,256]{2,1,0:T(8,128)(2,1)}, bf16[2,560,256]{2,1,0:T(8,128)(2,1)}, u32[]{:S(2)}, u32[]{:S(2)}) collective-permute-start(bf16[2,560,256]{2,1,0:T(8,128)(2,1)} %fusion.2.refs_1_), channel_id=1, source_target_pairs={{0,1},{1,0},{2,3},{3,2},{4,5},{5,4},{6,7},{7,6},{8,9},{9,8},{10,11... | collective-permute-start | bytes 1720328 | tf_op jit(solution)/shard_map/ppermute | solution.py:462
  240.0 10.9 %collective-permute-start.27 = (bf16[2,4,160,192]{3,2,1,0:T(8,128)(2,1)}, bf16[2,4,160,192]{3,2,1,0:T(8,128)(2,1)}, u32[]{:S(2)}, u32[]{:S(2)}) collective-permute-start(bf16[2,4,160,192]{3,2,1,0:T(8,128)(2,1)} %get-tuple-element.130._), channel_id=1, source_target_pairs={{0,8},{4,20},{8,0},{12,28},{16,24},{20,4},{24,16},{28,12},{1,9},{5... | collective-permute-start | bytes 1474568 | tf_op jit(solution)/shard_map/ppermute | solution.py:462
  253.2 8.1 %collective-permute-start.30 = (f32[8,640]{1,0:T(8,128)S(1)}, f32[8,640]{1,0:T(8,128)S(1)}, u32[]{:S(2)}, u32[]{:S(2)}) collective-permute-start(f32[8,640]{1,0:T(8,128)S(1)} %add.237), channel_id=1, source_target_pairs={{0,8},{4,12},{8,0},{12,4},{16,24},{20,28},{24,16},{28,20},{1,9},{5... | collective-permute-start | bytes 61448 | tf_op jit(solution)/shard_map/ppermute | solution.py:462
  256.8 7.2 %collective-permute-start.29 = (bf16[4,160,192]{2,1,0:T(8,128)(2,1)S(1)}, bf16[4,160,192]{2,1,0:T(8,128)(2,1)S(1)}, u32[]{:S(2)}, u32[]{:S(2)}) collective-permute-start(bf16[4,160,192]{2,1,0:T(8,128)(2,1)S(1)} %fusion.10), channel_id=1, source_target_pairs={{0,16},{4,12},{8,24},{12,4},{16,0},{20,28},{24,8},{28,20},{1,17},{... | collective-permute-start | bytes 737288 | tf_op jit(solution)/shard_map/ppermute | solution.py:462
  258.8 18.1 %collective-permute-start.36 = (bf16[560,256]{1,0:T(8,128)(2,1)S(1)}, bf16[560,256]{1,0:T(8,128)(2,1)S(1)}, u32[]{:S(2)}, u32[]{:S(2)}) collective-permute-start(bf16[560,256]{1,0:T(8,128)(2,1)S(1)} %fusion.6), channel_id=1, source_target_pairs={{0,2},{1,3},{2,0},{3,1},{4,6},{5,7},{6,4},{7,5},{8,10},{9,11},{10,... | collective-permute-start | bytes 860168 | tf_op jit(solution)/shard_map/ppermute | solution.py:462
  265.1 8.6 %collective-permute-start.37 = (f32[8,640]{1,0:T(8,128)S(1)}, f32[8,640]{1,0:T(8,128)S(1)}, u32[]{:S(2)}, u32[]{:S(2)}) collective-permute-start(f32[8,640]{1,0:T(8,128)S(1)} %add_add_fusion.1), channel_id=1, source_target_pairs={{0,1},{1,0},{2,3},{3,2},{4,5},{5,4},{6,7},{7,6},{8,9},{9,8},{10,11... | collective-permute-start | bytes 61448 | tf_op jit(solution)/shard_map/ppermute | solution.py:462
  265.4 10.2 %collective-permute-start.38 = (f32[8,640]{1,0:T(8,128)S(1)}, f32[8,640]{1,0:T(8,128)S(1)}, u32[]{:S(2)}, u32[]{:S(2)}) collective-permute-start(f32[8,640]{1,0:T(8,128)S(1)} %add_add_fusion.1), channel_id=1, source_target_pairs={{0,2},{1,3},{2,0},{3,1},{4,6},{5,7},{6,4},{7,5},{8,10},{9,11},{10,... | collective-permute-start | bytes 61448 | tf_op jit(solution)/shard_map/ppermute | solution.py:462
  268.8 6.8 %collective-permute-start.39 = (f32[8,640]{1,0:T(8,128)S(1)}, f32[8,640]{1,0:T(8,128)S(1)}, u32[]{:S(2)}, u32[]{:S(2)}) collective-permute-start(f32[8,640]{1,0:T(8,128)S(1)} %add_add_fusion.1), channel_id=1, source_target_pairs={{0,3},{1,2},{2,1},{3,0},{4,7},{5,6},{6,5},{7,4},{8,11},{9,10},{10,... | collective-permute-start | bytes 61448 | tf_op jit(solution)/shard_map/ppermute | solution.py:462
  270.5 9.7 %collective-permute-start.33 = (bf16[160,192]{1,0:T(8,128)(2,1)S(1)}, bf16[160,192]{1,0:T(8,128)(2,1)S(1)}, u32[]{:S(2)}, u32[]{:S(2)}) collective-permute-start(bf16[160,192]{1,0:T(8,128)(2,1)S(1)} %get-tuple-element.145), channel_id=1, source_target_pairs={{0,3},{1,2},{2,1},{3,0},{4,7},{5,6},{6,5},{7,4},{8,11},{9,10},{10,... | collective-permute-start | bytes 184328 | tf_op jit(solution)/shard_map/ppermute | solution.py:462
  (24 other events, 384.7 us)
